TPU v7x, 512 devices: a whole 4x4x16 slice. The times are simulated.
512 devices in a mesh: lon: 32 (over x_lo, z), lat: 16 (over y, x_hi, core).
Axes of the slice: x: 4 (x_hi: 2, x_lo: 2; x = x_hi * 2 + x_lo), y: 4, z: 16, core: 2. Of those that a mesh axis runs over, the one named last changes fastest.
Arguments:
- heat_state: float32 [64, 128, 8192], P(None, 'lat', 'lon'), may hold values from -6 to 6
- salt_anomaly: float32 [64, 128, 8192], P(None, 'lat', 'lon'), may hold values from -6 to 6
- zonal_current: float32 [64, 128, 8192], P(None, 'lat', 'lon'), may hold values from -4 to 4
- meridional_current: float32 [64, 128, 8192], P(None, 'lat', 'lon'), may hold values from -4 to 4
- ocean_layer_number: int32 [128, 8192], P('lat', 'lon'), may hold values from 0 to 64, as said below
- sea_elevation: float32 [128, 8192], P('lat', 'lon'), may hold values from -6 to 6
- zonal_mean_current: float32 [128, 8192], P('lat', 'lon'), may hold values from -3 to 3
- meridional_mean_current: float32 [128, 8192], P('lat', 'lon'), may hold values from -3 to 3
- first_layer_matrix: bfloat16 [128, 256], replicated, may hold values from -0.5 to 0.5
- second_layer_matrix: bfloat16 [256, 64], replicated, may hold values from -0.375 to 0.375
Outputs:
- next_heat_state: float32 [64, 128, 8192], P(None, 'lat', 'lon')
- next_salt_anomaly: float32 [64, 128, 8192], P(None, 'lat', 'lon')
- height_next: float32 [128, 8192], P('lat', 'lon')
- east_next: float32 [128, 8192], P('lat', 'lon')
- north_next: float32 [128, 8192], P('lat', 'lon')
Inputs may be any that keep to these rules, and one draw needn't show every extreme that they name: `ocean_layer_number`: tiles of 8 rows by 32 columns, aligned, are, except the tile holding row 0 and column 0, either all land (no wet levels) or ocean with independent depths; some columns are fully deep and some are land.
All inputs are finite; a program needn't handle non-finite values.
Results may differ from a plain program's by a relative error of at most 0.0003.
Values sent between devices are 32-bit elements; how exact they have to be, the bound alone decides.
A program may use at most 64 MiB of HBM per device.

v0:
```python
import math

import jax
import jax.numpy as jnp
from jax import lax
from jax.sharding import PartitionSpec as P

SUBSTEPS = 4


ADVECT = 0.1
SMOOTHING = 0.1
GRAVITY = 0.3
SPREADING = 0.3
BUOYANCY = 0.5
THERMAL = 0.2
HALINE = 0.15
MIXING_MAX = 0.45


def with_halo(shard, sides, width, wrap):
    for axis, dim in sides:
        count, length = (lax.axis_size(axis), shard.shape[dim])
        up = [(i, (i + 1) % count) for i in range(count if wrap else count - 1)]
        down = [(j, i) for i, j in up]
        last = lax.slice_in_dim(shard, length - width, length, axis=dim)
        first = lax.slice_in_dim(shard, 0, width, axis=dim)
        before = lax.ppermute(last, axis, up)
        after = lax.ppermute(first, axis, down)
        shard = jnp.concatenate([before, shard, after], axis=dim)
    return shard


def level_mask(seafloor_matrix, layer_number):
    level_axis = lax.broadcasted_iota(jnp.float32, (layer_number,) + seafloor_matrix.shape, 0)
    return (level_axis < seafloor_matrix[None]).astype(jnp.float32)


def face_flux(lower, upper, speed_lower, speed_upper, shared):
    return shared * (
        ADVECT * 0.25 * (speed_lower + speed_upper) * (lower + upper) - SMOOTHING * (upper - lower)
    )


def sideways_share(tracer, zonal_flow_rate, meridional_rate, ocean_layer_flags):
    centre = tracer[:, 1:-1, 1:-1]
    interior_slice = ocean_layer_flags[:, 1:-1, 1:-1]
    east_face = face_flux(
        centre,
        tracer[:, 1:-1, 2:],
        zonal_flow_rate[:, 1:-1, 1:-1],
        zonal_flow_rate[:, 1:-1, 2:],
        interior_slice * ocean_layer_flags[:, 1:-1, 2:],
    )
    west_face = face_flux(
        tracer[:, 1:-1, :-2],
        centre,
        zonal_flow_rate[:, 1:-1, :-2],
        zonal_flow_rate[:, 1:-1, 1:-1],
        ocean_layer_flags[:, 1:-1, :-2] * interior_slice,
    )
    north_face = face_flux(
        centre,
        tracer[:, 2:, 1:-1],
        meridional_rate[:, 1:-1, 1:-1],
        meridional_rate[:, 2:, 1:-1],
        interior_slice * ocean_layer_flags[:, 2:, 1:-1],
    )
    south_face = face_flux(
        tracer[:, :-2, 1:-1],
        centre,
        meridional_rate[:, :-2, 1:-1],
        meridional_rate[:, 1:-1, 1:-1],
        ocean_layer_flags[:, :-2, 1:-1] * interior_slice,
    )
    return centre - interior_slice * (east_face - west_face + north_face - south_face)


def upright_share(tracer, diffusivity_factor):
    vertical_flux = diffusivity_factor[:-1] * (tracer[1:] - tracer[:-1])
    zero_layer = jnp.zeros_like(tracer[:1])
    return (
        tracer
        + jnp.concatenate([vertical_flux, zero_layer], 0)
        - jnp.concatenate([zero_layer, vertical_flux], 0)
    )


def contract(weight, inputs):
    return lax.dot_general(
        weight, inputs, (((0,), (0,)), ((), ())), preferred_element_type=jnp.float32
    )


def vertical_change(bordered_matrix, first_layer_matrix, second_layer_matrix):
    layer_number = (bordered_matrix.shape[0] - 1) // 4
    heat_state = bordered_matrix[:layer_number]
    salt_anomaly = bordered_matrix[layer_number : 2 * layer_number]
    zonal_flow_rate = bordered_matrix[2 * layer_number : 3 * layer_number]
    meridional_rate = bordered_matrix[3 * layer_number : 4 * layer_number]
    ocean_layer_flags = level_mask(bordered_matrix[4 * layer_number], layer_number)
    thermal_border = sideways_share(heat_state, zonal_flow_rate, meridional_rate, ocean_layer_flags)
    brine_neighbour = sideways_share(
        salt_anomaly, zonal_flow_rate, meridional_rate, ocean_layer_flags
    )
    interior_slice = ocean_layer_flags[:, 1:-1, 1:-1]
    row_count = interior_slice.shape[1]
    column_count = interior_slice.shape[2]
    network_entries = jnp.concatenate(
        [thermal_border * interior_slice, brine_neighbour * interior_slice], 0
    )
    network_entries = network_entries.reshape(2 * layer_number, row_count * column_count).astype(
        jnp.bfloat16
    )
    hidden = jnp.tanh(contract(first_layer_matrix, network_entries)).astype(jnp.bfloat16)
    logits = contract(second_layer_matrix, hidden).reshape(layer_number, row_count, column_count)
    below = jnp.concatenate([interior_slice[1:], jnp.zeros_like(interior_slice[:1])], 0)
    diffusivity_factor = MIXING_MAX * jax.nn.sigmoid(logits) * interior_slice * below
    return (
        upright_share(thermal_border, diffusivity_factor),
        upright_share(brine_neighbour, diffusivity_factor),
    )


def buoyancy_of(bordered_matrix):
    layer_number = (bordered_matrix.shape[0] - 1) // 4
    ocean_layer_flags = level_mask(bordered_matrix[4 * layer_number], layer_number)
    density = (
        THERMAL * bordered_matrix[:layer_number]
        - HALINE * bordered_matrix[layer_number : 2 * layer_number]
    )
    return jnp.sum(ocean_layer_flags * density, axis=0) * (1.0 / math.sqrt(layer_number))


def forcing(buoyancy):
    east_force = -BUOYANCY * 0.5 * (buoyancy[1:-1, 2:] - buoyancy[1:-1, :-2])
    north_force = -BUOYANCY * 0.5 * (buoyancy[2:, 1:-1] - buoyancy[:-2, 1:-1])
    return (east_force, north_force)


def trimmed(field):
    return field[1:-1, 1:-1]


def substep(topmost_layer, layer_number):
    height = topmost_layer[0]
    east_flow = topmost_layer[1]
    north_flow = topmost_layer[2]
    east_force = topmost_layer[3]
    north_force = topmost_layer[4]
    seafloor_matrix = topmost_layer[5]
    wet_cells = (seafloor_matrix > 0).astype(jnp.float32)
    column_depth = seafloor_matrix / layer_number
    east_new = trimmed(wet_cells) * (
        trimmed(east_flow)
        - GRAVITY * 0.5 * (height[1:-1, 2:] - height[1:-1, :-2])
        + trimmed(east_force)
    )
    north_new = trimmed(wet_cells) * (
        trimmed(north_flow)
        - GRAVITY * 0.5 * (height[2:, 1:-1] - height[:-2, 1:-1])
        + trimmed(north_force)
    )
    east_carry = trimmed(column_depth) * east_new
    north_carry = trimmed(column_depth) * north_new
    divergence = (
        east_carry[1:-1, 2:]
        - east_carry[1:-1, :-2]
        + north_carry[2:, 1:-1]
        - north_carry[:-2, 1:-1]
    )
    height_new = trimmed(trimmed(wet_cells)) * (
        trimmed(trimmed(height)) - SPREADING * 0.5 * divergence
    )
    return jnp.stack(
        [
            height_new,
            trimmed(east_new),
            trimmed(north_new),
            trimmed(trimmed(east_force)),
            trimmed(trimmed(north_force)),
            trimmed(trimmed(seafloor_matrix)),
        ]
    )


def local(
    heat_state,
    salt_anomaly,
    zonal_current,
    meridional_current,
    ocean_layer_number,
    sea_elevation,
    zonal_mean_current,
    meridional_mean_current,
    first_layer_matrix,
    second_layer_matrix,
):
    layer_number = heat_state.shape[0]
    seafloor_matrix = ocean_layer_number.astype(jnp.float32)
    joined_tracers = jnp.concatenate(
        [heat_state, salt_anomaly, zonal_current, meridional_current, seafloor_matrix[None]], 0
    )
    lon_padded = with_halo(joined_tracers, (("lon", 2),), 1, True)
    bordered_matrix = with_halo(lon_padded, (("lat", 1),), 1, False)
    next_heat_state, next_salt_anomaly = vertical_change(
        bordered_matrix, first_layer_matrix, second_layer_matrix
    )
    east_force, north_force = forcing(buoyancy_of(bordered_matrix))
    topmost_layer = jnp.stack(
        [
            sea_elevation,
            zonal_mean_current,
            meridional_mean_current,
            east_force,
            north_force,
            seafloor_matrix,
        ]
    )
    for substep_index in range(SUBSTEPS):
        surface_wrapped = with_halo(topmost_layer, (("lon", 2),), 2, True)
        surface_framed = with_halo(surface_wrapped, (("lat", 1),), 2, False)
        topmost_layer = substep(surface_framed, layer_number)
    return (
        next_heat_state,
        next_salt_anomaly,
        topmost_layer[0],
        topmost_layer[1],
        topmost_layer[2],
    )


def solution(mesh):
    return jax.shard_map(
        local,
        mesh=mesh,
        in_specs=(
            P(None, "lat", "lon"),
            P(None, "lat", "lon"),
            P(None, "lat", "lon"),
            P(None, "lat", "lon"),
            P("lat", "lon"),
            P("lat", "lon"),
            P("lat", "lon"),
            P("lat", "lon"),
            P(),
            P(),
        ),
        out_specs=(
            P(None, "lat", "lon"),
            P(None, "lat", "lon"),
            P("lat", "lon"),
            P("lat", "lon"),
            P("lat", "lon"),
        ),
        check_vma=False,
    )
```

profile of v0, /device:TPU:1, one launch (start us, length us, event | category | flops | bytes accessed | tf_op | source)
XLA Modules:
  0.0 132.2 jit_solution(4499588537136986554)
XLA Ops:
  3.1 1.3 %fusion.73 = (f32[257,8,1]{2,1,0:T(8,128)}, f32[257,8,1]{2,1,0:T(8,128)S(1)}) fusion(f32[257,8,256]{2,1,0:T(8,128)S(1)} %constant_dynamic-update-slice_fusion), kind=kLoop, calls=%fused_computation.232 | loop fusion | bytes 32896 | tf_op jit(solution)/shard_map/slice | solution.py:26
  4.4 1.7 %copy.63 = f32[257,8,1]{0,1,2:T(8,128)S(1)} copy(f32[257,8,1]{2,1,0:T(8,128)} %get-tuple-element.32) | data formatting | bytes 16448 | tf_op jit(solution)/shard_map/slice | solution.py:26
  6.1 4.4 %collective-permute-start = (f32[257,8,1]{0,1,2:T(8,128)S(1)}, f32[257,8,1]{0,1,2:T(8,128)S(1)}, u32[]{:S(2)}, u32[]{:S(2)}) collective-permute-start(f32[257,8,1]{0,1,2:T(8,128)S(1)} %copy.63), channel_id=1, source_target_pairs={{0,16},{16,32},{32,48},{48,64},{64,80},{80,96},{96,112},{112,128},... | collective-permute-start | bytes 24680 | tf_op jit(solution)/shard_map/ppermute | solution.py:28
  11.1 10.4 %collective-permute-start.1 = (f32[257,8,1]{0,1,2:T(8,128)S(1)}, f32[257,8,1]{0,1,2:T(8,128)S(1)}, u32[]{:S(2)}, u32[]{:S(2)}) collective-permute-start(f32[257,8,1]{0,1,2:T(8,128)S(1)} %copy.64), channel_id=1, source_target_pairs={{16,0},{32,16},{48,32},{64,48},{80,64},{96,80},{112,96},{128,112},... | collective-permute-start | bytes 24680 | tf_op jit(solution)/shard_map/ppermute | solution.py:29
  22.3 1.5 %copy.66 = f32[257,8,1]{2,1,0:T(8,128)} copy(f32[257,8,1]{0,1,2:T(8,128)S(1)} %collective-permute-done.1) | data formatting | bytes 16448 | tf_op jit(solution)/shard_map/ppermute | solution.py:29
  23.8 3.8 %pad_maximum_fusion.19 = (f32[257,1,258]{2,1,0:T(1,128)S(1)}, f32[257,1,258]{2,1,0:T(1,128)S(1)}) fusion(f32[257,8,1]{2,1,0:T(8,128)} %copy.66, f32[257,8,256]{2,1,0:T(8,128)S(1)} %constant_dynamic-update-slice_fusion, f32[257,8,1]{2,1,0:T(8,128)S(1)} %copy.65), kind=kLoop, calls=%fused_computation.57 | loop fusion | flops 265224 | bytes 2652240 | tf_op jit(solution)/shard_map/slice | solution.py:26
  27.7 5.9 %collective-permute-start.2 = (f32[257,1,258]{2,0,1:T(8,128)S(1)}, f32[257,1,258]{2,0,1:T(8,128)S(1)}, u32[]{:S(2)}, u32[]{:S(2)}) collective-permute-start(f32[257,1,258]{2,0,1:T(8,128)S(1)} %copy.67), channel_id=1, source_target_pairs={{0,1},{1,2},{2,3},{3,4},{4,5},{5,6},{6,7},{7,8},{8,9},{9,10},{10,1... | collective-permute-start | bytes 795680 | tf_op jit(solution)/shard_map/ppermute | solution.py:28
  33.7 1.9 %collective-permute-start.3 = (f32[257,1,258]{2,0,1:T(8,128)S(1)}, f32[257,1,258]{2,0,1:T(8,128)S(1)}, u32[]{:S(2)}, u32[]{:S(2)}) collective-permute-start(f32[257,1,258]{2,0,1:T(8,128)S(1)} %copy.68), channel_id=1, source_target_pairs={{1,0},{2,1},{3,2},{4,3},{5,4},{6,5},{7,6},{8,7},{9,8},{10,9},{11,1... | collective-permute-start | bytes 795680 | tf_op jit(solution)/shard_map/ppermute | solution.py:29
  35.6 2.8 %collective-permute-done.2 = f32[257,1,258]{2,0,1:T(8,128)S(1)} collective-permute-done((f32[257,1,258]{2,0,1:T(8,128)S(1)}, f32[257,1,258]{2,0,1:T(8,128)S(1)}, u32[]{:S(2)}, u32[]{:S(2)}) %collective-permute-start.2) | collective-permute-done | bytes 265256 | tf_op jit(solution)/shard_map/ppermute | solution.py:28
  38.9 5.9 %collective-permute-done.3 = f32[257,1,258]{2,0,1:T(8,128)S(1)} collective-permute-done((f32[257,1,258]{2,0,1:T(8,128)S(1)}, f32[257,1,258]{2,0,1:T(8,128)S(1)}, u32[]{:S(2)}, u32[]{:S(2)}) %collective-permute-start.3) | collective-permute-done | bytes 265256 | tf_op jit(solution)/shard_map/ppermute | solution.py:29
  45.3 1.6 %fusion.8 = f32[10,258]{1,0:T(8,128)S(1)} fusion(f32[257,1,258]{2,1,0:T(1,128)S(1)} %copy.70, f32[257,1,258]{2,1,0:T(1,128)S(1)} %copy.69, f32[257,8,1]{2,1,0:T(8,128)S(1)} %copy-done.3, f32[257,8,256]{2,1,0:T(8,128)S(1)} %constant_dynamic-update-slice_fusion, f32[257,8,1]{2,1,0:T(8,128)S(1)} %copy.65, f32[10,258]{1,0:T(8,128)S(1)} %maximum_bitcast_fusion), kind=kLoop, calls=%fused_computation.11 | loop fusion | flops 2309100 | bytes 2672880 | tf_op jit(solution)/shard_map/reduce_sum | solution.py:132
  47.1 2.0 %collective-permute-start.4 = (f32[6,8,2]{2,1,0:T(8,128)S(1)}, f32[6,8,2]{2,1,0:T(8,128)S(1)}, u32[]{:S(2)}, u32[]{:S(2)}) collective-permute-start(f32[6,8,2]{2,1,0:T(8,128)S(1)} %get-tuple-element.82), channel_id=1, source_target_pairs={{0,16},{16,32},{32,48},{48,64},{64,80},{80,96},{96,112},{112,128},... | collective-permute-start | bytes 1160 | tf_op jit(solution)/shard_map/ppermute | solution.py:28
  49.2 6.0 %collective-permute-start.5 = (f32[6,8,2]{2,1,0:T(8,128)S(1)}, f32[6,8,2]{2,1,0:T(8,128)S(1)}, u32[]{:S(2)}, u32[]{:S(2)}) collective-permute-start(f32[6,8,2]{2,1,0:T(8,128)S(1)} %get-tuple-element.83), channel_id=1, source_target_pairs={{16,0},{32,16},{48,32},{64,48},{80,64},{96,80},{112,96},{128,112},... | collective-permute-start | bytes 1160 | tf_op jit(solution)/shard_map/ppermute | solution.py:29
  56.2 3.2 %collective-permute-start.6 = (f32[6,2,260]{2,1,0:T(2,128)S(1)}, f32[6,2,260]{2,1,0:T(2,128)S(1)}, u32[]{:S(2)}, u32[]{:S(2)}) collective-permute-start(f32[6,2,260]{2,1,0:T(2,128)S(1)} %get-tuple-element.66), channel_id=1, source_target_pairs={{0,1},{1,2},{2,3},{3,4},{4,5},{5,6},{6,7},{7,8},{8,9},{9,10},{10,1... | collective-permute-start | bytes 37448 | tf_op jit(solution)/shard_map/ppermute | solution.py:28
  59.5 1.9 %collective-permute-start.7 = (f32[6,2,260]{2,1,0:T(2,128)S(1)}, f32[6,2,260]{2,1,0:T(2,128)S(1)}, u32[]{:S(2)}, u32[]{:S(2)}) collective-permute-start(f32[6,2,260]{2,1,0:T(2,128)S(1)} %get-tuple-element.67), channel_id=1, source_target_pairs={{1,0},{2,1},{3,2},{4,3},{5,4},{6,5},{7,6},{8,7},{9,8},{10,9},{11,1... | collective-permute-start | bytes 37448 | tf_op jit(solution)/shard_map/ppermute | solution.py:29
  61.5 4.5 %collective-permute-done.7 = f32[6,2,260]{2,1,0:T(2,128)S(1)} collective-permute-done((f32[6,2,260]{2,1,0:T(2,128)S(1)}, f32[6,2,260]{2,1,0:T(2,128)S(1)}, u32[]{:S(2)}, u32[]{:S(2)}) %collective-permute-start.7) | collective-permute-done | bytes 12512 | tf_op jit(solution)/shard_map/ppermute | solution.py:29
  66.9 1.9 %collective-permute-start.8 = (f32[6,8,2]{2,1,0:T(8,128)S(1)}, f32[6,8,2]{2,1,0:T(8,128)S(1)}, u32[]{:S(2)}, u32[]{:S(2)}) collective-permute-start(f32[6,8,2]{2,1,0:T(8,128)S(1)} %get-tuple-element.80), channel_id=1, source_target_pairs={{0,16},{16,32},{32,48},{48,64},{64,80},{80,96},{96,112},{112,128},... | collective-permute-start | bytes 1160 | tf_op jit(solution)/shard_map/ppermute | solution.py:28
  68.8 5.6 %collective-permute-start.9 = (f32[6,8,2]{2,1,0:T(8,128)S(1)}, f32[6,8,2]{2,1,0:T(8,128)S(1)}, u32[]{:S(2)}, u32[]{:S(2)}) collective-permute-start(f32[6,8,2]{2,1,0:T(8,128)S(1)} %get-tuple-element.81), channel_id=1, source_target_pairs={{16,0},{32,16},{48,32},{64,48},{80,64},{96,80},{112,96},{128,112},... | collective-permute-start | bytes 1160 | tf_op jit(solution)/shard_map/ppermute | solution.py:29
  74.5 3.8 %multiply_convert_fusion.1 = (bf16[64,8,256]{2,1,0:T(8,128)(2,1)S(1)}, f32[64,8,256]{2,1,0:T(8,128)}) fusion(f32[64,10,258]{2,1,0:T(8,128)S(1)} %fusion.9, f32[64,8,256]{2,1,0:T(8,128)S(1)} %copy-done.10, f32[257,8,1]{2,1,0:T(8,128)S(1)} %copy-done.3, f32[257,8,256]{2,1,0:T(8,128)S(1)} %constant_dynamic-update-slice_fusion, f32[257,8,1]{2,1,0:T(8,128)S(1)} %copy.65, ...), kind=kLoop, calls=%fused_computation.47 | loop fusion | flops 7733248 | bytes 7632976 | tf_op jit(solution)/shard_map/convert.1
  78.4 2.8 %collective-permute-start.10 = (f32[6,2,260]{2,1,0:T(2,128)S(1)}, f32[6,2,260]{2,1,0:T(2,128)S(1)}, u32[]{:S(2)}, u32[]{:S(2)}) collective-permute-start(f32[6,2,260]{2,1,0:T(2,128)S(1)} %get-tuple-element.64), channel_id=1, source_target_pairs={{0,1},{1,2},{2,3},{3,4},{4,5},{5,6},{6,7},{7,8},{8,9},{9,10},{10,1... | collective-permute-start | bytes 37448 | tf_op jit(solution)/shard_map/ppermute | solution.py:28
  81.2 1.9 %collective-permute-start.11 = (f32[6,2,260]{2,1,0:T(2,128)S(1)}, f32[6,2,260]{2,1,0:T(2,128)S(1)}, u32[]{:S(2)}, u32[]{:S(2)}) collective-permute-start(f32[6,2,260]{2,1,0:T(2,128)S(1)} %get-tuple-element.65), channel_id=1, source_target_pairs={{1,0},{2,1},{3,2},{4,3},{5,4},{6,5},{7,6},{8,7},{9,8},{10,9},{11,1... | collective-permute-start | bytes 37448 | tf_op jit(solution)/shard_map/ppermute | solution.py:29
  83.2 3.8 %multiply_convert_fusion = (bf16[64,8,256]{2,1,0:T(8,128)(2,1)S(1)}, f32[64,8,256]{2,1,0:T(8,128)}) fusion(f32[64,10,258]{2,1,0:T(8,128)S(1)} %fusion.9, f32[64,8,256]{2,1,0:T(8,128)S(1)} %copy-done.11, f32[257,8,1]{2,1,0:T(8,128)S(1)} %copy-done.3, f32[257,8,256]{2,1,0:T(8,128)S(1)} %constant_dynamic-update-slice_fusion, f32[257,8,1]{2,1,0:T(8,128)S(1)} %copy.65, ...), kind=kLoop, calls=%fused_computation.45 | loop fusion | flops 7733248 | bytes 7632976 | tf_op jit(solution)/shard_map/convert.2
  88.6 1.9 %collective-permute-start.12 = (f32[6,8,2]{2,1,0:T(8,128)S(1)}, f32[6,8,2]{2,1,0:T(8,128)S(1)}, u32[]{:S(2)}, u32[]{:S(2)}) collective-permute-start(f32[6,8,2]{2,1,0:T(8,128)S(1)} %get-tuple-element.78), channel_id=1, source_target_pairs={{0,16},{16,32},{32,48},{48,64},{64,80},{80,96},{96,112},{112,128},... | collective-permute-start | bytes 1160 | tf_op jit(solution)/shard_map/ppermute | solution.py:28
  90.6 5.7 %collective-permute-start.13 = (f32[6,8,2]{2,1,0:T(8,128)S(1)}, f32[6,8,2]{2,1,0:T(8,128)S(1)}, u32[]{:S(2)}, u32[]{:S(2)}) collective-permute-start(f32[6,8,2]{2,1,0:T(8,128)S(1)} %get-tuple-element.79), channel_id=1, source_target_pairs={{16,0},{32,16},{48,32},{64,48},{80,64},{96,80},{112,96},{128,112},... | collective-permute-start | bytes 1160 | tf_op jit(solution)/shard_map/ppermute | solution.py:29
  97.1 5.5 %collective-permute-start.14 = (f32[6,2,260]{2,1,0:T(2,128)S(1)}, f32[6,2,260]{2,1,0:T(2,128)S(1)}, u32[]{:S(2)}, u32[]{:S(2)}) collective-permute-start(f32[6,2,260]{2,1,0:T(2,128)S(1)} %get-tuple-element.62), channel_id=1, source_target_pairs={{0,1},{1,2},{2,3},{3,4},{4,5},{5,6},{6,7},{7,8},{8,9},{9,10},{10,1... | collective-permute-start | bytes 37448 | tf_op jit(solution)/shard_map/ppermute | solution.py:28
  102.6 1.9 %collective-permute-start.15 = (f32[6,2,260]{2,1,0:T(2,128)S(1)}, f32[6,2,260]{2,1,0:T(2,128)S(1)}, u32[]{:S(2)}, u32[]{:S(2)}) collective-permute-start(f32[6,2,260]{2,1,0:T(2,128)S(1)} %get-tuple-element.63), channel_id=1, source_target_pairs={{1,0},{2,1},{3,2},{4,3},{5,4},{6,5},{7,6},{8,7},{9,8},{10,9},{11,1... | collective-permute-start | bytes 37448 | tf_op jit(solution)/shard_map/ppermute | solution.py:29
  106.5 2.6 %collective-permute-done.15 = f32[6,2,260]{2,1,0:T(2,128)S(1)} collective-permute-done((f32[6,2,260]{2,1,0:T(2,128)S(1)}, f32[6,2,260]{2,1,0:T(2,128)S(1)}, u32[]{:S(2)}, u32[]{:S(2)}) %collective-permute-start.15) | collective-permute-done | bytes 12512 | tf_op jit(solution)/shard_map/ppermute | solution.py:29
  110.0 1.9 %collective-permute-start.16 = (f32[6,8,2]{2,1,0:T(8,128)S(1)}, f32[6,8,2]{2,1,0:T(8,128)S(1)}, u32[]{:S(2)}, u32[]{:S(2)}) collective-permute-start(f32[6,8,2]{2,1,0:T(8,128)S(1)} %get-tuple-element.76), channel_id=1, source_target_pairs={{0,16},{16,32},{32,48},{48,64},{64,80},{80,96},{96,112},{112,128},... | collective-permute-start | bytes 1160 | tf_op jit(solution)/shard_map/ppermute | solution.py:28
  111.9 5.5 %collective-permute-start.17 = (f32[6,8,2]{2,1,0:T(8,128)S(1)}, f32[6,8,2]{2,1,0:T(8,128)S(1)}, u32[]{:S(2)}, u32[]{:S(2)}) collective-permute-start(f32[6,8,2]{2,1,0:T(8,128)S(1)} %get-tuple-element.77), channel_id=1, source_target_pairs={{16,0},{32,16},{48,32},{64,48},{80,64},{96,80},{112,96},{128,112},... | collective-permute-start | bytes 1160 | tf_op jit(solution)/shard_map/ppermute | solution.py:29
  118.4 4.0 %collective-permute-start.18 = (f32[6,2,260]{2,1,0:T(2,128)S(1)}, f32[6,2,260]{2,1,0:T(2,128)S(1)}, u32[]{:S(2)}, u32[]{:S(2)}) collective-permute-start(f32[6,2,260]{2,1,0:T(2,128)S(1)} %get-tuple-element.60), channel_id=1, source_target_pairs={{0,1},{1,2},{2,3},{3,4},{4,5},{5,6},{6,7},{7,8},{8,9},{9,10},{10,1... | collective-permute-start | bytes 37448 | tf_op jit(solution)/shard_map/ppermute | solution.py:28
  122.4 1.9 %collective-permute-start.19 = (f32[6,2,260]{2,1,0:T(2,128)S(1)}, f32[6,2,260]{2,1,0:T(2,128)S(1)}, u32[]{:S(2)}, u32[]{:S(2)}) collective-permute-start(f32[6,2,260]{2,1,0:T(2,128)S(1)} %get-tuple-element.61), channel_id=1, source_target_pairs={{1,0},{2,1},{3,2},{4,3},{5,4},{6,5},{7,6},{8,7},{9,8},{10,9},{11,1... | collective-permute-start | bytes 37448 | tf_op jit(solution)/shard_map/ppermute | solution.py:29
  125.5 4.3 %collective-permute-done.19 = f32[6,2,260]{2,1,0:T(2,128)S(1)} collective-permute-done((f32[6,2,260]{2,1,0:T(2,128)S(1)}, f32[6,2,260]{2,1,0:T(2,128)S(1)}, u32[]{:S(2)}, u32[]{:S(2)}) %collective-permute-start.19) | collective-permute-done | bytes 12512 | tf_op jit(solution)/shard_map/ppermute | solution.py:29
  (122 shorter events, 16.6 us)
Async XLA Ops:
  0.6 103.9 %copy-start = (bf16[128,256]{1,0:T(8,128)(2,1)S(1)}, bf16[128,256]{1,0:T(8,128)(2,1)}, u32[]{:S(2)}) copy-start(bf16[128,256]{1,0:T(8,128)(2,1)} %param.18) | copy-start | bytes 196612
  4.4 17.1 %copy-start.13 = (f32[8,256]{1,0:T(8,128)S(1)}, f32[8,256]{1,0:T(8,128)}, u32[]{:S(2)}) copy-start(f32[8,256]{1,0:T(8,128)} %param.15) | copy-start | bytes 24580
  6.1 15.4 %collective-permute-start = (f32[257,8,1]{0,1,2:T(8,128)S(1)}, f32[257,8,1]{0,1,2:T(8,128)S(1)}, u32[]{:S(2)}, u32[]{:S(2)}) collective-permute-start(f32[257,8,1]{0,1,2:T(8,128)S(1)} %copy.63), channel_id=1, source_target_pairs={{0,16},{16,32},{32,48},{48,64},{64,80},{80,96},{96,112},{112,128},... | collective-permute-start | bytes 24680 | tf_op jit(solution)/shard_map/ppermute | solution.py:28
  11.1 11.2 %collective-permute-start.1 = (f32[257,8,1]{0,1,2:T(8,128)S(1)}, f32[257,8,1]{0,1,2:T(8,128)S(1)}, u32[]{:S(2)}, u32[]{:S(2)}) collective-permute-start(f32[257,8,1]{0,1,2:T(8,128)S(1)} %copy.64), channel_id=1, source_target_pairs={{16,0},{32,16},{48,32},{64,48},{80,64},{96,80},{112,96},{128,112},... | collective-permute-start | bytes 24680 | tf_op jit(solution)/shard_map/ppermute | solution.py:29
  27.7 8.0 %copy-start.15 = (f32[8,256]{1,0:T(8,128)S(1)}, f32[8,256]{1,0:T(8,128)}, u32[]{:S(2)}) copy-start(f32[8,256]{1,0:T(8,128)} %param.17) | copy-start | bytes 24580
  27.7 17.5 %copy-start.3 = (f32[257,8,1]{2,1,0:T(8,128)S(1)}, f32[257,8,1]{2,1,0:T(8,128)}, u32[]{:S(2)}) copy-start(f32[257,8,1]{2,1,0:T(8,128)} %copy.66) | copy-start | bytes 24676
  27.7 10.7 %collective-permute-start.2 = (f32[257,1,258]{2,0,1:T(8,128)S(1)}, f32[257,1,258]{2,0,1:T(8,128)S(1)}, u32[]{:S(2)}, u32[]{:S(2)}) collective-permute-start(f32[257,1,258]{2,0,1:T(8,128)S(1)} %copy.67), channel_id=1, source_target_pairs={{0,1},{1,2},{2,3},{3,4},{4,5},{5,6},{6,7},{7,8},{8,9},{9,10},{10,1... | collective-permute-start | bytes 795680 | tf_op jit(solution)/shard_map/ppermute | solution.py:28
  33.7 11.1 %collective-permute-start.3 = (f32[257,1,258]{2,0,1:T(8,128)S(1)}, f32[257,1,258]{2,0,1:T(8,128)S(1)}, u32[]{:S(2)}, u32[]{:S(2)}) collective-permute-start(f32[257,1,258]{2,0,1:T(8,128)S(1)} %copy.68), channel_id=1, source_target_pairs={{1,0},{2,1},{3,2},{4,3},{5,4},{6,5},{7,6},{8,7},{9,8},{10,9},{11,1... | collective-permute-start | bytes 795680 | tf_op jit(solution)/shard_map/ppermute | solution.py:29
  46.8 27.6 %copy-start.7 = (f32[64,8,256]{2,1,0:T(8,128)S(1)}, f32[64,8,256]{2,1,0:T(8,128)}, u32[]{:S(2)}) copy-start(f32[64,8,256]{2,1,0:T(8,128)} %param.12) | copy-start | bytes 1572868
  46.9 27.6 %copy-start.9 = (f32[64,8,256]{2,1,0:T(8,128)S(1)}, f32[64,8,256]{2,1,0:T(8,128)}, u32[]{:S(2)}) copy-start(f32[64,8,256]{2,1,0:T(8,128)} %param.13) | copy-start | bytes 1572868
  46.9 27.6 %copy-start.10 = (f32[64,8,256]{2,1,0:T(8,128)S(1)}, f32[64,8,256]{2,1,0:T(8,128)}, u32[]{:S(2)}) copy-start(f32[64,8,256]{2,1,0:T(8,128)} %param.10) | copy-start | bytes 1572868
  47.1 8.1 %collective-permute-start.4 = (f32[6,8,2]{2,1,0:T(8,128)S(1)}, f32[6,8,2]{2,1,0:T(8,128)S(1)}, u32[]{:S(2)}, u32[]{:S(2)}) collective-permute-start(f32[6,8,2]{2,1,0:T(8,128)S(1)} %get-tuple-element.82), channel_id=1, source_target_pairs={{0,16},{16,32},{32,48},{48,64},{64,80},{80,96},{96,112},{112,128},... | collective-permute-start | bytes 1160 | tf_op jit(solution)/shard_map/ppermute | solution.py:28
  49.2 7.0 %collective-permute-start.5 = (f32[6,8,2]{2,1,0:T(8,128)S(1)}, f32[6,8,2]{2,1,0:T(8,128)S(1)}, u32[]{:S(2)}, u32[]{:S(2)}) collective-permute-start(f32[6,8,2]{2,1,0:T(8,128)S(1)} %get-tuple-element.83), channel_id=1, source_target_pairs={{16,0},{32,16},{48,32},{64,48},{80,64},{96,80},{112,96},{128,112},... | collective-permute-start | bytes 1160 | tf_op jit(solution)/shard_map/ppermute | solution.py:29
  56.2 5.3 %collective-permute-start.6 = (f32[6,2,260]{2,1,0:T(2,128)S(1)}, f32[6,2,260]{2,1,0:T(2,128)S(1)}, u32[]{:S(2)}, u32[]{:S(2)}) collective-permute-start(f32[6,2,260]{2,1,0:T(2,128)S(1)} %get-tuple-element.66), channel_id=1, source_target_pairs={{0,1},{1,2},{2,3},{3,4},{4,5},{5,6},{6,7},{7,8},{8,9},{9,10},{10,1... | collective-permute-start | bytes 37448 | tf_op jit(solution)/shard_map/ppermute | solution.py:28
  59.5 6.6 %collective-permute-start.7 = (f32[6,2,260]{2,1,0:T(2,128)S(1)}, f32[6,2,260]{2,1,0:T(2,128)S(1)}, u32[]{:S(2)}, u32[]{:S(2)}) collective-permute-start(f32[6,2,260]{2,1,0:T(2,128)S(1)} %get-tuple-element.67), channel_id=1, source_target_pairs={{1,0},{2,1},{3,2},{4,3},{5,4},{6,5},{7,6},{8,7},{9,8},{10,9},{11,1... | collective-permute-start | bytes 37448 | tf_op jit(solution)/shard_map/ppermute | solution.py:29
  61.5 21.6 %copy-start.1 = (f32[64,10,258]{2,1,0:T(8,128)}, f32[64,10,258]{2,1,0:T(8,128)S(1)}, u32[]{:S(2)}) copy-start(f32[64,10,258]{2,1,0:T(8,128)S(1)} %fusion.9) | copy-start | bytes 1981444
  66.9 11.4 %collective-permute-start.8 = (f32[6,8,2]{2,1,0:T(8,128)S(1)}, f32[6,8,2]{2,1,0:T(8,128)S(1)}, u32[]{:S(2)}, u32[]{:S(2)}) collective-permute-start(f32[6,8,2]{2,1,0:T(8,128)S(1)} %get-tuple-element.80), channel_id=1, source_target_pairs={{0,16},{16,32},{32,48},{48,64},{64,80},{80,96},{96,112},{112,128},... | collective-permute-start | bytes 1160 | tf_op jit(solution)/shard_map/ppermute | solution.py:28
  68.8 14.4 %copy-start.11 = (f32[64,8,256]{2,1,0:T(8,128)S(1)}, f32[64,8,256]{2,1,0:T(8,128)}, u32[]{:S(2)}) copy-start(f32[64,8,256]{2,1,0:T(8,128)} %param.11) | copy-start | bytes 1572868
  68.8 9.5 %collective-permute-start.9 = (f32[6,8,2]{2,1,0:T(8,128)S(1)}, f32[6,8,2]{2,1,0:T(8,128)S(1)}, u32[]{:S(2)}, u32[]{:S(2)}) collective-permute-start(f32[6,8,2]{2,1,0:T(8,128)S(1)} %get-tuple-element.81), channel_id=1, source_target_pairs={{16,0},{32,16},{48,32},{64,48},{80,64},{96,80},{112,96},{128,112},... | collective-permute-start | bytes 1160 | tf_op jit(solution)/shard_map/ppermute | solution.py:29
  78.4 8.6 %collective-permute-start.10 = (f32[6,2,260]{2,1,0:T(2,128)S(1)}, f32[6,2,260]{2,1,0:T(2,128)S(1)}, u32[]{:S(2)}, u32[]{:S(2)}) collective-permute-start(f32[6,2,260]{2,1,0:T(2,128)S(1)} %get-tuple-element.64), channel_id=1, source_target_pairs={{0,1},{1,2},{2,3},{3,4},{4,5},{5,6},{6,7},{7,8},{8,9},{9,10},{10,1... | collective-permute-start | bytes 37448 | tf_op jit(solution)/shard_map/ppermute | solution.py:28
  81.2 6.6 %collective-permute-start.11 = (f32[6,2,260]{2,1,0:T(2,128)S(1)}, f32[6,2,260]{2,1,0:T(2,128)S(1)}, u32[]{:S(2)}, u32[]{:S(2)}) collective-permute-start(f32[6,2,260]{2,1,0:T(2,128)S(1)} %get-tuple-element.65), channel_id=1, source_target_pairs={{1,0},{2,1},{3,2},{4,3},{5,4},{6,5},{7,6},{8,7},{9,8},{10,9},{11,1... | collective-permute-start | bytes 37448 | tf_op jit(solution)/shard_map/ppermute | solution.py:29
  87.9 16.6 %copy-start.16 = (bf16[256,64]{0,1:T(8,128)(2,1)S(1)}, bf16[256,64]{0,1:T(8,128)(2,1)}, u32[]{:S(2)}) copy-start(bf16[256,64]{0,1:T(8,128)(2,1)} %param.19) | copy-start | bytes 98308
  88.6 8.1 %collective-permute-start.12 = (f32[6,8,2]{2,1,0:T(8,128)S(1)}, f32[6,8,2]{2,1,0:T(8,128)S(1)}, u32[]{:S(2)}, u32[]{:S(2)}) collective-permute-start(f32[6,8,2]{2,1,0:T(8,128)S(1)} %get-tuple-element.78), channel_id=1, source_target_pairs={{0,16},{16,32},{32,48},{48,64},{64,80},{80,96},{96,112},{112,128},... | collective-permute-start | bytes 1160 | tf_op jit(solution)/shard_map/ppermute | solution.py:28
  90.6 6.4 %collective-permute-start.13 = (f32[6,8,2]{2,1,0:T(8,128)S(1)}, f32[6,8,2]{2,1,0:T(8,128)S(1)}, u32[]{:S(2)}, u32[]{:S(2)}) collective-permute-start(f32[6,8,2]{2,1,0:T(8,128)S(1)} %get-tuple-element.79), channel_id=1, source_target_pairs={{16,0},{32,16},{48,32},{64,48},{80,64},{96,80},{112,96},{128,112},... | collective-permute-start | bytes 1160 | tf_op jit(solution)/shard_map/ppermute | solution.py:29
  97.1 9.4 %collective-permute-start.14 = (f32[6,2,260]{2,1,0:T(2,128)S(1)}, f32[6,2,260]{2,1,0:T(2,128)S(1)}, u32[]{:S(2)}, u32[]{:S(2)}) collective-permute-start(f32[6,2,260]{2,1,0:T(2,128)S(1)} %get-tuple-element.62), channel_id=1, source_target_pairs={{0,1},{1,2},{2,3},{3,4},{4,5},{5,6},{6,7},{7,8},{8,9},{9,10},{10,1... | collective-permute-start | bytes 37448 | tf_op jit(solution)/shard_map/ppermute | solution.py:28
  102.6 6.6 %collective-permute-start.15 = (f32[6,2,260]{2,1,0:T(2,128)S(1)}, f32[6,2,260]{2,1,0:T(2,128)S(1)}, u32[]{:S(2)}, u32[]{:S(2)}) collective-permute-start(f32[6,2,260]{2,1,0:T(2,128)S(1)} %get-tuple-element.63), channel_id=1, source_target_pairs={{1,0},{2,1},{3,2},{4,3},{5,4},{6,5},{7,6},{8,7},{9,8},{10,9},{11,1... | collective-permute-start | bytes 37448 | tf_op jit(solution)/shard_map/ppermute | solution.py:29
  106.1 11.3 %copy-start.4 = (f32[64,8,256]{2,1,0:T(8,128)S(1)}, f32[64,8,256]{2,1,0:T(8,128)}, u32[]{:S(2)}) copy-start(f32[64,8,256]{2,1,0:T(8,128)} %get-tuple-element.27) | copy-start | bytes 1572868
  106.1 11.3 %copy-start.5 = (f32[64,8,256]{2,1,0:T(8,128)S(1)}, f32[64,8,256]{2,1,0:T(8,128)}, u32[]{:S(2)}) copy-start(f32[64,8,256]{2,1,0:T(8,128)} %get-tuple-element.29) | copy-start | bytes 1572868
  110.0 7.6 %collective-permute-start.16 = (f32[6,8,2]{2,1,0:T(8,128)S(1)}, f32[6,8,2]{2,1,0:T(8,128)S(1)}, u32[]{:S(2)}, u32[]{:S(2)}) collective-permute-start(f32[6,8,2]{2,1,0:T(8,128)S(1)} %get-tuple-element.76), channel_id=1, source_target_pairs={{0,16},{16,32},{32,48},{48,64},{64,80},{80,96},{96,112},{112,128},... | collective-permute-start | bytes 1160 | tf_op jit(solution)/shard_map/ppermute | solution.py:28
  111.9 6.4 %collective-permute-start.17 = (f32[6,8,2]{2,1,0:T(8,128)S(1)}, f32[6,8,2]{2,1,0:T(8,128)S(1)}, u32[]{:S(2)}, u32[]{:S(2)}) collective-permute-start(f32[6,8,2]{2,1,0:T(8,128)S(1)} %get-tuple-element.77), channel_id=1, source_target_pairs={{16,0},{32,16},{48,32},{64,48},{80,64},{96,80},{112,96},{128,112},... | collective-permute-start | bytes 1160 | tf_op jit(solution)/shard_map/ppermute | solution.py:29
  118.4 7.1 %collective-permute-start.18 = (f32[6,2,260]{2,1,0:T(2,128)S(1)}, f32[6,2,260]{2,1,0:T(2,128)S(1)}, u32[]{:S(2)}, u32[]{:S(2)}) collective-permute-start(f32[6,2,260]{2,1,0:T(2,128)S(1)} %get-tuple-element.60), channel_id=1, source_target_pairs={{0,1},{1,2},{2,3},{3,4},{4,5},{5,6},{6,7},{7,8},{8,9},{9,10},{10,1... | collective-permute-start | bytes 37448 | tf_op jit(solution)/shard_map/ppermute | solution.py:28
  122.4 7.4 %collective-permute-start.19 = (f32[6,2,260]{2,1,0:T(2,128)S(1)}, f32[6,2,260]{2,1,0:T(2,128)S(1)}, u32[]{:S(2)}, u32[]{:S(2)}) collective-permute-start(f32[6,2,260]{2,1,0:T(2,128)S(1)} %get-tuple-element.61), channel_id=1, source_target_pairs={{1,0},{2,1},{3,2},{4,3},{5,4},{6,5},{7,6},{8,7},{9,8},{10,9},{11,1... | collective-permute-start | bytes 37448 | tf_op jit(solution)/shard_map/ppermute | solution.py:29
  (5 other events, 15.2 us)
where the time goes:
time: 134 us; the launch traced here: 132 us
  starting transfers between devices  76.3 us (57%)
  waiting for transfers between devices  23.1 us (17%)
  other arithmetic  17.1 us (13%)
  local copies, waits for them, and re-layouts  13.3 us (10%)
  between operations  1.42 us (1%)
    ppermute x10, starting transfers between devices, with_halo(): after = lax.ppermute(first, axis, down)  42.8 us
    ppermute x10, starting transfers between devices, with_halo(): before = lax.ppermute(last, axis, up)  33.6 us
    ppermute x10, waiting for transfers between devices, with_halo(): after = lax.ppermute(first, axis, down)  20.3 us
    another operation x2, other arithmetic  7.66 us
    slice x5, other arithmetic, with_halo(): last = lax.slice_in_dim(shard, length - width, length, axis=dim)  4.27 us
    unnamed x54, local copies, waits for them, and re-layouts  4.01 us
    slice x7, local copies, waits for them, and re-layouts, with_halo(): last = lax.slice_in_dim(shard, length - width, length, axis=dim)  3.38 us
    ppermute x10, waiting for transfers between devices, with_halo(): before = lax.ppermute(last, axis, up)  2.85 us
  transfers between devices with their start and end apart: 20, of which 10 were waited for; matrix products, arithmetic and copies ran while one was open for 9% of the time, Pallas kernels for 0%

commit v1 on v0

v1 whole, which is shorter than its diff:
```python
import functools

import jax
import jax.numpy as jnp
from jax import lax
from jax.experimental import pallas as pl
from jax.experimental.pallas import tpu as pltpu
from jax.sharding import PartitionSpec as P

MESH = pl.DeviceIdType.MESH
SUBSTEPS = 4
ADVECT = 0.1 * 0.25
SMOOTHING = 0.1
GRAVITY = 0.3 * 0.5
SPREADING = 0.3 * 0.5
BUOYANCY = 0.5 * 0.5
THERMAL = 0.2
HALINE = 0.15
MIXING_MAX = 0.45
LIMIT = 40 * 2**20
PERIOD = 16
LEVELS, ROWS, COLS, HID = 64, 8, 256, 256
GROUPS = LEVELS // 8
TILE = 128
U, T, S, V = range(4)
HEIGHT, EAST, NORTH, DEPTH, BUOYANT = range(5)
FIELDS = 5
E, W, N, S_, NE, SE, NW, SW = range(8)


def turn(x, shift, axis):
    return pltpu.roll(x, shift % x.shape[axis], axis)


def lanes_of(shape):
    return lax.broadcasted_iota(jnp.int32, shape, 1)


def levels_of(cols):
    return lax.broadcasted_iota(jnp.int32, (LEVELS, cols), 0).astype(jnp.float32)


def tall(block):
    return jnp.concatenate([block] * GROUPS, 0)


def network(w1_t, w2_t, thermal, saline):
    entries = jnp.concatenate([thermal, saline], 0).astype(jnp.bfloat16)
    hidden = jnp.tanh(jnp.dot(w1_t, entries, preferred_element_type=jnp.float32))
    return jnp.dot(
        w2_t, hidden.astype(jnp.bfloat16), preferred_element_type=jnp.float32
    )


def mixing(logits):
    return (0.5 * MIXING_MAX) * (1.0 + jnp.tanh(0.5 * logits))


def settle(tracer, kappa):
    flux = kappa * (turn(tracer, -1, 0) - tracer)
    return tracer + flux - turn(flux, 1, 0)


def face(lower, upper, speed, shared):
    return jnp.where(
        shared, ADVECT * speed * (lower + upper) - SMOOTHING * (upper - lower), 0.0
    )


def packed(vreg_of, slots, lane):
    where = lanes_of((8, TILE))
    halves = []
    for r in range(2):
        total = None
        for g in range(4):
            part = None
            for a in range(slots):
                for j in range(ROWS):
                    target = 32 * g + 8 * a + j
                    moved = turn(vreg_of(a, j, 2 * g + r), target - lane, 1)
                    base = jnp.zeros_like(moved) if part is None else part
                    part = jnp.where(where == target, moved, base)
            total = part if total is None else total + part
        halves.append(total)
    return jnp.concatenate(halves, 0)


def unfolded(folded):
    return jnp.concatenate([turn(folded, -32 * g, 1) for g in range(4)], 0)


def edge_flux(lower, upper):
    first = lanes_of(lower.shape) % 32 < 8
    total, both = lower + upper, lower * upper
    speed = jnp.where(first, turn(total, -16, 1), turn(total, -8, 1))
    shared = jnp.where(first, turn(both, -24, 1), turn(both, -16, 1))
    return shared * (ADVECT * speed * total - SMOOTHING * (upper - lower))


def exchange(
    nlon, nlat,
    t, s, u, v, depth, height, east, north, w1, w2,
    out_t, out_s, out_surface,
    x, side, surface, depth_int, w1_in, w1_t, w2_t, deep, deep_east, lon_out, lon_in, corner_in,
    load_sem, row_send, row_recv, send_sem, recv_sem, seam_sem, ready_sem,
):
    lon, lat = lax.axis_index("lon"), lax.axis_index("lat")
    z = lax.rem(lon, PERIOD)
    early, late, before = z == 0, z == PERIOD - 1, z == PERIOD - 2
    has_n, has_s = lat < nlat - 1, lat > 0
    sides = has_n.astype(jnp.int32) + has_s.astype(jnp.int32)
    to_east, to_west = lax.rem(lon + 1, nlon), lax.rem(lon + nlon - 1, nlon)
    device = {
        E: {"lon": to_east},
        W: {"lon": to_west},
        N: {"lat": lat + 1},
        S_: {"lat": lat - 1},
        NE: {"lon": to_east, "lat": lat + 1},
        SE: {"lon": to_east, "lat": lat - 1},
        NW: {"lon": to_west, "lat": lat + 1},
        SW: {"lon": to_west, "lat": lat - 1},
    }
    there = {E: True, W: True, N: has_n, NE: has_n, NW: has_n, S_: has_s, SE: has_s, SW: has_s}

    def signal(sem, way, also=True):
        @pl.when(jnp.logical_and(there[way], also))
        def _():
            pl.semaphore_signal(sem, inc=1, device_id=device[way], device_id_type=MESH)

    local = pltpu.make_async_copy
    plane = pl.ds(ROWS, ROWS)
    first = [local(depth, depth_int, load_sem.at[0])]
    first += [
        local(f, surface.at[k, plane], load_sem.at[1 + k])
        for k, f in enumerate((height, east, north))
    ]
    for c in first:
        c.start()

    def load_half(half):
        cut = pl.ds(half * TILE, TILE)
        for k, f in ((T, t), (S, s), (U, u)):
            for j in range(ROWS):
                local(f.at[:, j, cut], x.at[k, j + 1, :, cut], load_sem.at[4 + half]).start()

    def wait_half(half):
        whole = x.at[pl.ds(0, 3), pl.ds(1, ROWS), :, pl.ds(half * TILE, TILE)]
        local(whole, whole, load_sem.at[4 + half]).wait()

    load_half(1)

    barrier = pltpu.get_barrier_semaphore()
    signal(barrier, W)
    signal(barrier, NW)
    signal(barrier, SW)
    usual = jnp.logical_not(late)
    signal(barrier, E, usual)
    signal(barrier, N, usual)
    signal(barrier, S_, usual)
    inner = jnp.logical_and(usual, jnp.logical_not(before))
    signal(barrier, NE, inner)
    signal(barrier, SE, inner)

    load_half(0)
    for j in range(ROWS):
        local(v.at[:, j, :], x.at[V, j + 1], load_sem.at[6]).start()
    weights = [local(w1, w1_in, load_sem.at[7]), local(w2, w2_t, load_sem.at[8])]
    for c in weights:
        c.start()

    expected = jnp.where(early, 1 + 2 * sides, jnp.where(late, 2 + sides, 2 + 3 * sides))
    pl.semaphore_wait(barrier, expected)
    for way in (E, NE, SE):
        signal(seam_sem, way, late)
    for way in (NE, SE):
        signal(ready_sem, way, before)

    remote = pltpu.make_async_remote_copy

    def row_copies(way):
        source, target = (ROWS - 1, 0) if way == N else (0, ROWS + 1)
        k = way - N
        return [
            remote(f.at[:, source, :], x.at[a, target], row_send.at[3 * k + i], row_recv.at[1 - k],
                   device_id=device[way], device_id_type=MESH)
            for i, (a, f) in enumerate(((T, t), (S, s), (V, v)))
        ]

    opposite = {E: W, W: E, N: S_, S_: N, NE: SW, SW: NE, NW: SE, SE: NW}
    lon_slot = {E: 0, W: 1}
    corner_slot = {NE: 0, SE: 1, NW: 2, SW: 3}
    surface_rows = {N: pl.ds(2 * ROWS, ROWS), S_: pl.ds(0, ROWS)}
    tail = pl.ds(16, 8)

    def message(way):
        if way in lon_slot:
            src, dst = lon_out.at[lon_slot[way]], lon_in.at[lon_slot[opposite[way]]]
        elif way in corner_slot:
            src = lon_out.at[0 if way in (NE, SE) else 1, tail]
            dst = corner_in.at[corner_slot[opposite[way]]]
        else:
            src, dst = surface.at[:, plane], surface.at[:, surface_rows[opposite[way]]]
        return remote(src, dst, send_sem.at[way], recv_sem.at[opposite[way]],
                      device_id=device[way], device_id_type=MESH)

    def send(way, also=True):
        @pl.when(jnp.logical_and(there[way], also))
        def _():
            message(way).start()

    def send_rows(also):
        for way in (N, S_):

            @pl.when(jnp.logical_and(there[way], also))
            def _(way=way):
                for c in row_copies(way):
                    c.start()

    send_rows(usual)

    @pl.when(jnp.logical_not(has_s))
    def _():
        x[:, 0] = jnp.zeros((4, LEVELS, COLS), jnp.float32)
        surface[:, 0:ROWS] = jnp.zeros((FIELDS, ROWS, COLS), jnp.float32)
        corner_in[1] = jnp.zeros((8, TILE), jnp.float32)
        corner_in[3] = jnp.zeros((8, TILE), jnp.float32)

    @pl.when(jnp.logical_not(has_n))
    def _():
        x[:, ROWS + 1] = jnp.zeros((4, LEVELS, COLS), jnp.float32)
        surface[:, 2 * ROWS : 3 * ROWS] = jnp.zeros((FIELDS, ROWS, COLS), jnp.float32)
        corner_in[0] = jnp.zeros((8, TILE), jnp.float32)
        corner_in[2] = jnp.zeros((8, TILE), jnp.float32)

    for c in first:
        c.wait()
    deeps = depth_int[...].astype(jnp.float32)
    surface[DEPTH, plane] = deeps
    beside = jnp.where(lanes_of((ROWS, COLS)) == COLS - 1, 0.0, turn(deeps, -1, 1))
    beside = jnp.minimum(deeps, beside)
    for j in range(ROWS):
        deep[j + 1] = jnp.broadcast_to(deeps[j : j + 1], (8, COLS))
        deep_east[j] = jnp.broadcast_to(beside[j : j + 1], (8, COLS))

    def pack_half(half):
        cut = pl.ds(half * TILE, TILE)
        edge = TILE - 1 if half else 0
        level = lax.broadcasted_iota(jnp.int32, (8, TILE), 0).astype(jnp.float32)
        where = lanes_of((8, TILE))

        def wet(j, q):
            return level + 8.0 * q < deep[j + 1, :, cut]

        def vreg(a, j, q):
            if a == 3:
                return jnp.where(wet(j, q), 1.0, 0.0)
            return x[(T, S, U)[a], j + 1, pl.ds(8 * q, 8), cut]

        lon_out[1 - half, 0:16] = packed(vreg, 4, edge)
        for j in range(ROWS):
            total = jnp.zeros((8, TILE), jnp.float32)
            for q in range(GROUPS):
                rows = pl.ds(8 * q, 8)
                density = THERMAL * x[T, j + 1, rows, cut] - HALINE * x[S, j + 1, rows, cut]
                total = total + jnp.where(wet(j, q), density, 0.0)
            surface[BUOYANT, ROWS + j : ROWS + j + 1, cut] = (LEVELS**-0.5) * jnp.sum(total, 0, keepdims=True)
        kept = (where >= TILE - 8) if half else (where < 8)
        lon_out[1 - half, 16:24] = sum(
            turn(jnp.where(kept, surface[f, plane, cut], 0.0), 16 * f, 1)
            for f in range(FIELDS)
        )

    wait_half(1)
    pack_half(1)
    for way in (E, NE, SE):
        send(way)
    wait_half(0)
    pack_half(0)
    send(W, jnp.logical_not(early))
    middle = jnp.logical_and(usual, jnp.logical_not(early))
    send(NW, middle)
    send(SW, middle)
    send(N, usual)
    send(S_, usual)

    @pl.when(late)
    def _():
        pl.semaphore_wait(ready_sem, 2 * sides)

    send_rows(late)
    for way in (NW, SW, N, S_):
        send(way, late)

    for c in weights:
        c.wait()
    w1_t[...] = w1_in[...].astype(jnp.float32).T.astype(jnp.bfloat16)
    all_v = x.at[V, pl.ds(1, ROWS)]
    local(all_v, all_v, load_sem.at[6]).wait()

    def row(j):
        level = levels_of(COLS)
        speed = x[U, j + 1]
        speed = speed + turn(speed, -1, 1)
        here, above, below = deep[j + 1], deep[j + 2], deep[j]
        open_east = level < tall(deep_east[j])
        open_north = level < tall(jnp.minimum(here, above))
        open_south = level < tall(jnp.minimum(here, below))
        wet = level < tall(here)
        wet_below = level + 1.0 < tall(here)
        speed_north = x[V, j + 1] + x[V, j + 2]
        speed_south = x[V, j + 1] + x[V, j]

        def lateral(k):
            own = x[k, j + 1]
            flux = face(own, turn(own, -1, 1), speed, open_east)
            return own - (
                flux
                - turn(flux, 1, 1)
                + face(own, x[k, j + 2], speed_north, open_north)
                - face(x[k, j], own, speed_south, open_south)
            )

        thermal, saline = lateral(T), lateral(S)
        side[0, j] = thermal
        side[1, j] = saline
        logits = network(
            w1_t[...], w2_t[...], jnp.where(wet, thermal, 0.0), jnp.where(wet, saline, 0.0)
        )
        kappa = jnp.where(wet_below, mixing(logits), 0.0)
        out_t[j] = settle(thermal, kappa)
        out_s[j] = settle(saline, kappa)

    pl.loop(1, ROWS - 1)(row)

    @pl.when(early)
    def _():
        pl.semaphore_wait(seam_sem, 1 + sides)

    signal(ready_sem, NW, early)
    signal(ready_sem, SW, early)
    for way in (W, NW, SW):
        send(way, early)

    for way in (N, S_):

        @pl.when(there[way])
        def _(way=way):
            k = way - N
            rows = x.at[pl.ds(T, 3), ROWS + 1 if way == N else 0]
            local(rows, rows, row_recv.at[k]).wait()
            message(opposite[way]).wait_recv()

    deep[0] = jnp.broadcast_to(surface[DEPTH, ROWS - 1 : ROWS], (8, COLS))
    deep[ROWS + 1] = jnp.broadcast_to(surface[DEPTH, 2 * ROWS : 2 * ROWS + 1], (8, COLS))

    @pl.loop(0, 2)
    def _(i):
        row(i * (ROWS - 1))

    def side_pack(half):
        cut = pl.ds(half * TILE, TILE)
        return packed(
            lambda a, j, q: side[a, j, pl.ds(8 * q, 8), cut],
            2,
            TILE - 1 if half else 0,
        )

    part_east, part_west = side_pack(1), side_pack(0)

    for way in (E, W, NE, SE, NW, SW):

        @pl.when(there[way])
        def _(way=way):
            message(opposite[way]).wait_recv()

    own_east, own_west = lon_out[0, 0:16], lon_out[1, 0:16]
    from_east, from_west = lon_in[0, 0:16], lon_in[1, 0:16]
    at_east = part_east - edge_flux(own_east, from_east)
    at_west = part_west + edge_flux(from_west, own_west)
    lane16 = lanes_of((16, TILE))
    first_slot = lane16 % 32 < 8
    thermal = unfolded(jnp.where(first_slot, at_west, turn(at_east, 8, 1)))
    saline = unfolded(jnp.where(first_slot, turn(at_west, -8, 1), at_east))
    wet = unfolded(jnp.where(first_slot, turn(own_west, -24, 1), turn(own_east, -16, 1)))
    lane = lanes_of((LEVELS, TILE))
    wet = jnp.where(lane < 16, wet, 0.0)
    wet_below = jnp.where(levels_of(TILE) < LEVELS - 1.0, turn(wet, -1, 0), 0.0)
    logits = network(w1_t[...], w2_t[...], thermal * wet, saline * wet)
    kappa = mixing(logits) * wet * wet_below
    for out, tracer in ((out_t, thermal), (out_s, saline)):
        new = settle(tracer, kappa)
        for j in range(ROWS):
            out[j, :, 0:TILE] = jnp.where(lane == 0, turn(new, -j, 1), out[j, :, 0:TILE])
            out[j, :, TILE:] = jnp.where(lane == TILE - 1, turn(new, TILE - 1 - 8 - j, 1), out[j, :, TILE:])

    third = jnp.concatenate(
        [
            corner_in[1] + corner_in[3],
            lon_in[0, 16:24] + lon_in[1, 16:24],
            corner_in[0] + corner_in[2],
        ],
        0,
    )
    where = lanes_of((3 * ROWS, TILE))
    around = jnp.logical_or(where < 8, where >= TILE - 8)
    field = [
        jnp.concatenate([surface[f], jnp.where(around, turn(third, -16 * f, 1), 0.0)], 1)
        for f in range(FIELDS)
    ]
    h, e, n, d, b = field
    land = d <= 0.0
    column = d * (1.0 / LEVELS)

    def eastward(a):
        return turn(a, -1, 1) - turn(a, 1, 1)

    def northward(a):
        return turn(a, -1, 0) - turn(a, 1, 0)

    east_force, north_force = -BUOYANCY * eastward(b), -BUOYANCY * northward(b)
    for _ in range(SUBSTEPS):
        e = jnp.where(land, 0.0, e - GRAVITY * eastward(h) + east_force)
        n = jnp.where(land, 0.0, n - GRAVITY * northward(h) + north_force)
        h = jnp.where(land, 0.0, h - SPREADING * (eastward(column * e) + northward(column * n)))
    for k, a in enumerate((h, e, n)):
        out_surface[k] = a[ROWS : 2 * ROWS, 0:COLS]

    for way in (N, S_):

        @pl.when(there[way])
        def _(way=way):
            for c in row_copies(way):
                c.wait_send()

    for way in range(8):

        @pl.when(there[way])
        def _(way=way):
            message(way).wait_send()


def deliver(t, s, surface, out_t, out_s, height, east, north, sem):
    copies = []
    for src, dst in ((t, out_t), (s, out_s)):
        copies += [(src.at[j], dst.at[:, j, :]) for j in range(ROWS)]
    copies += [(surface.at[k], dst) for k, dst in enumerate((height, east, north))]
    copies = [pltpu.make_async_copy(a, b, sem.at[i]) for i, (a, b) in enumerate(copies)]
    for c in copies:
        c.start()
    for c in copies:
        c.wait()


def solution(mesh):
    nlon, nlat = mesh.shape["lon"], mesh.shape["lat"]
    f32, bf16 = jnp.float32, jnp.bfloat16
    rows = jax.ShapeDtypeStruct((ROWS, LEVELS, COLS), f32)
    block = jax.ShapeDtypeStruct((LEVELS, ROWS, COLS), f32)
    plane = jax.ShapeDtypeStruct((ROWS, COLS), f32)
    anywhere, vmem = pl.BlockSpec(memory_space=pl.ANY), pl.BlockSpec(memory_space=pltpu.VMEM)
    dma = pltpu.SemaphoreType.DMA

    def local(*args):
        args = [pltpu.with_memory_space_constraint(a, pltpu.HBM) for a in (*args[:-1], args[-1].T)]
        columns = pl.pallas_call(
            functools.partial(exchange, nlon, nlat),
            out_shape=(rows, rows, jax.ShapeDtypeStruct((3, ROWS, COLS), f32)),
            in_specs=[anywhere] * 10,
            out_specs=(vmem,) * 3,
            scratch_shapes=[
                pltpu.VMEM((4, ROWS + 2, LEVELS, COLS), f32),
                pltpu.VMEM((2, ROWS, LEVELS, COLS), f32),
                pltpu.VMEM((FIELDS, 3 * ROWS, COLS), f32),
                pltpu.VMEM((ROWS, COLS), jnp.int32),
                pltpu.VMEM((2 * LEVELS, HID), bf16),
                pltpu.VMEM((HID, 2 * LEVELS), bf16),
                pltpu.VMEM((LEVELS, HID), bf16),
                pltpu.VMEM((ROWS + 2, 8, COLS), f32),
                pltpu.VMEM((ROWS, 8, COLS), f32),
                pltpu.VMEM((2, 24, TILE), f32),
                pltpu.VMEM((2, 24, TILE), f32),
                pltpu.VMEM((4, 8, TILE), f32),
                dma((9,)),
                dma((6,)),
                dma((2,)),
                dma((8,)),
                dma((8,)),
                pltpu.SemaphoreType.REGULAR,
                pltpu.SemaphoreType.REGULAR,
            ],
            compiler_params=pltpu.CompilerParams(
                collective_id=0, has_side_effects=True, vmem_limit_bytes=LIMIT
            ),
        )(*args)
        return pl.pallas_call(
            deliver,
            out_shape=(block, block, plane, plane, plane),
            in_specs=[vmem] * 3,
            out_specs=(anywhere,) * 5,
            scratch_shapes=[dma((2 * ROWS + 3,))],
            compiler_params=pltpu.CompilerParams(vmem_limit_bytes=LIMIT),
        )(*columns)

    split, flat = P(None, "lat", "lon"), P("lat", "lon")
    return jax.shard_map(
        local,
        mesh=mesh,
        in_specs=(split,) * 4 + (flat,) * 4 + (P(), P()),
        out_specs=(split, split, flat, flat, flat),
        check_vma=False,
    )
```

time: 134 us -> 20.3 us (0.15)
  the two profiles are of different devices: /device:TPU:1 before, /device:TPU:491 now
where the time goes in v1:
time: 20.3 us; the launch traced here: 20.1 us
  Pallas kernels  19.5 us (96%)
  between operations  0.64 us (3%)
    pallas_call x1, Pallas kernels, local(): pl.pallas_call(functools.partial(exchange, nlon, nlat), out_shape=(rows,...  18.3 us
    pallas_call x1, Pallas kernels, local(): pl.pallas_call(deliver, out_shape=(block, block, plane, plane, plane), in...  1.13 us

profile of v1, /device:TPU:491, one launch (start us, length us, event | category | flops | bytes accessed | tf_op | source)
XLA Modules:
  0.0 20.1 jit_solution(603663737510523276)
XLA Ops:
  0.6 18.3 %shard_map.137 = (f32[8,64,256]{2,1,0:T(8,128)S(1)}, f32[8,64,256]{2,1,0:T(8,128)S(1)}, f32[3,8,256]{2,1,0:T(8,128)S(1)}) custom-call(f32[64,8,256]{2,1,0:T(8,128)} %t.1, f32[64,8,256]{2,1,0:T(8,128)} %s.1, f32[64,8,256]{2,1,0:T(8,128)} %u.1, f32[64,8,256]{2,1,0:T(8,128)} %v.1, s32[8,256]{1,0:T(8,128)} %depth.1, f32[8,256]{1,0:T(8,128)} %height.1, ...), custom_call_target="tpu_custom_call" | custom-call | tf_op jit(solution)/shard_map/pallas_call | solution.py:465
  19.0 1.1 %shard_map.138 = (f32[64,8,256]{2,1,0:T(8,128)}, f32[64,8,256]{2,1,0:T(8,128)}, f32[8,256]{1,0:T(8,128)}, f32[8,256]{1,0:T(8,128)}, f32[8,256]{1,0:T(8,128)}) custom-call(f32[8,64,256]{2,1,0:T(8,128)S(1)} %get-tuple-element.8.t, f32[8,64,256]{2,1,0:T(8,128)S(1)} %get-tuple-element.9.s, f32[3,8,256]{2,1,0:T(8,128)S(1)} %get-tuple-element.10.surface), custom_call_target="tpu_custom_call" | custom-call | tf_op jit(solution)/shard_map/pallas_call | solution.py:495

commit v2 on v1

--- a/solution.py
+++ b/solution.py
@@ -23,13 +23,14 @@
 GROUPS = LEVELS // 8
 TILE = 128
 U, T, S, V = range(4)
-HEIGHT, EAST, NORTH, DEPTH, BUOYANT = range(5)
+HEIGHT, EAST, NORTH, BUOYANT, DEPTH = range(5)
 FIELDS = 5
 E, W, N, S_, NE, SE, NW, SW = range(8)
 
 
 def turn(x, shift, axis):
-    return pltpu.roll(x, shift % x.shape[axis], axis)
+    size = x.shape[axis]
+    return pltpu.roll(x, shift % size if isinstance(shift, int) else lax.rem(shift, size), axis)
 
 
 def lanes_of(shape):
@@ -67,7 +68,7 @@
     )
 
 
-def packed(vreg_of, slots, lane):
+def packed(vreg_of, slots, lane, rows):
     where = lanes_of((8, TILE))
     halves = []
     for r in range(2):
@@ -75,9 +76,9 @@
         for g in range(4):
             part = None
             for a in range(slots):
-                for j in range(ROWS):
+                for j in rows:
                     target = 32 * g + 8 * a + j
-                    moved = turn(vreg_of(a, j, 2 * g + r), target - lane, 1)
+                    moved = turn(vreg_of(a, j, 2 * g + r), target - lane + TILE, 1)
                     base = jnp.zeros_like(moved) if part is None else part
                     part = jnp.where(where == target, moved, base)
             total = part if total is None else total + part
@@ -102,7 +103,7 @@
     t, s, u, v, depth, height, east, north, w1, w2,
     out_t, out_s, out_surface,
     x, side, surface, depth_int, w1_in, w1_t, w2_t, deep, deep_east, lon_out, lon_in, corner_in,
-    load_sem, row_send, row_recv, send_sem, recv_sem, seam_sem, ready_sem,
+    load_sem, row_send, row_recv, depth_send, depth_recv, send_sem, recv_sem, seam_sem, ready_sem,
 ):
     lon, lat = lax.axis_index("lon"), lax.axis_index("lat")
     z = lax.rem(lon, PERIOD)
@@ -129,51 +130,61 @@
 
     local = pltpu.make_async_copy
     plane = pl.ds(ROWS, ROWS)
-    first = [local(depth, depth_int, load_sem.at[0])]
-    first += [
+    depth_load = local(depth, depth_int, load_sem.at[0])
+    surface_loads = [
         local(f, surface.at[k, plane], load_sem.at[1 + k])
         for k, f in enumerate((height, east, north))
     ]
-    for c in first:
+
+    def load_half(half, fields, sem):
+        cut = pl.ds(half * TILE, TILE)
+        for k, f in fields:
+            for j in range(ROWS):
+                local(f.at[:, j, cut], x.at[k, j + 1, :, cut], load_sem.at[sem]).start()
+
+    def wait_half(half, k, count, sem):
+        whole = x.at[pl.ds(k, count), pl.ds(1, ROWS), :, pl.ds(half * TILE, TILE)]
+        local(whole, whole, load_sem.at[sem]).wait()
+
+    depth_load.start()
+    load_half(1, ((T, t), (S, s)), 4)
+    for c in surface_loads:
         c.start()
-
-    def load_half(half):
-        cut = pl.ds(half * TILE, TILE)
-        for k, f in ((T, t), (S, s), (U, u)):
-            for j in range(ROWS):
-                local(f.at[:, j, cut], x.at[k, j + 1, :, cut], load_sem.at[4 + half]).start()
-
-    def wait_half(half):
-        whole = x.at[pl.ds(0, 3), pl.ds(1, ROWS), :, pl.ds(half * TILE, TILE)]
-        local(whole, whole, load_sem.at[4 + half]).wait()
-
-    load_half(1)
+    load_half(1, ((U, u),), 5)
 
     barrier = pltpu.get_barrier_semaphore()
     signal(barrier, W)
     signal(barrier, NW)
     signal(barrier, SW)
     usual = jnp.logical_not(late)
+    both = jnp.logical_and
+    place, half_one = lax.rem(lat, 4), lon < nlon // 2
+    north_first = jnp.where(place == 3, half_one, place != 1)
+    south_first = jnp.where(place == 0, jnp.logical_not(half_one), place == 2)
+    last_in_pair_n, last_in_pair_s = north_first, south_first
     signal(barrier, E, usual)
-    signal(barrier, N, usual)
-    signal(barrier, S_, usual)
-    inner = jnp.logical_and(usual, jnp.logical_not(before))
-    signal(barrier, NE, inner)
-    signal(barrier, SE, inner)
-
-    load_half(0)
+    signal(barrier, N, jnp.logical_or(usual, jnp.logical_not(last_in_pair_n)))
+    signal(barrier, S_, jnp.logical_or(usual, jnp.logical_not(last_in_pair_s)))
+    signal(barrier, NE, both(usual, jnp.logical_not(both(before, last_in_pair_n))))
+    signal(barrier, SE, both(usual, jnp.logical_not(both(before, last_in_pair_s))))
+
+    load_half(0, ((T, t), (S, s), (U, u)), 6)
     for j in range(ROWS):
-        local(v.at[:, j, :], x.at[V, j + 1], load_sem.at[6]).start()
-    weights = [local(w1, w1_in, load_sem.at[7]), local(w2, w2_t, load_sem.at[8])]
+        local(v.at[:, j, :], x.at[V, j + 1], load_sem.at[7]).start()
+    weights = [local(w1, w1_in, load_sem.at[8]), local(w2, w2_t, load_sem.at[9])]
     for c in weights:
         c.start()
 
-    expected = jnp.where(early, 1 + 2 * sides, jnp.where(late, 2 + sides, 2 + 3 * sides))
-    pl.semaphore_wait(barrier, expected)
-    for way in (E, NE, SE):
-        signal(seam_sem, way, late)
-    for way in (NE, SE):
-        signal(ready_sem, way, before)
+    count_n, count_s = has_n.astype(jnp.int32), has_s.astype(jnp.int32)
+    firsts = jnp.where(north_first, count_n, 0) + jnp.where(south_first, count_s, 0)
+    expected = jnp.where(early, 1 + 2 * sides, jnp.where(late, 2 + sides + 2 * firsts, 2 + 3 * sides))
+
+    @pl.when(usual)
+    def _():
+        pl.semaphore_wait(barrier, expected)
+
+    signal(ready_sem, NE, both(before, last_in_pair_n))
+    signal(ready_sem, SE, both(before, last_in_pair_s))
 
     remote = pltpu.make_async_remote_copy
 
@@ -199,9 +210,22 @@
             src = lon_out.at[0 if way in (NE, SE) else 1, tail]
             dst = corner_in.at[corner_slot[opposite[way]]]
         else:
-            src, dst = surface.at[:, plane], surface.at[:, surface_rows[opposite[way]]]
+            most = pl.ds(0, FIELDS - 1)
+            src, dst = surface.at[most, plane], surface.at[most, surface_rows[opposite[way]]]
         return remote(src, dst, send_sem.at[way], recv_sem.at[opposite[way]],
                       device_id=device[way], device_id_type=MESH)
+
+    def depth_message(way):
+        k = way - N
+        return remote(surface.at[DEPTH, plane], surface.at[DEPTH, surface_rows[opposite[way]]],
+                      depth_send.at[k], depth_recv.at[1 - k], device_id=device[way], device_id_type=MESH)
+
+    def send_depth(also):
+        for way in (N, S_):
+
+            @pl.when(jnp.logical_and(there[way], also))
+            def _(way=way):
+                depth_message(way).start()
 
     def send(way, also=True):
         @pl.when(jnp.logical_and(there[way], also))
@@ -232,8 +256,7 @@
         corner_in[0] = jnp.zeros((8, TILE), jnp.float32)
         corner_in[2] = jnp.zeros((8, TILE), jnp.float32)
 
-    for c in first:
-        c.wait()
+    depth_load.wait()
     deeps = depth_int[...].astype(jnp.float32)
     surface[DEPTH, plane] = deeps
     beside = jnp.where(lanes_of((ROWS, COLS)) == COLS - 1, 0.0, turn(deeps, -1, 1))
@@ -256,46 +279,69 @@
                 return jnp.where(wet(j, q), 1.0, 0.0)
             return x[(T, S, U)[a], j + 1, pl.ds(8 * q, 8), cut]
 
-        lon_out[1 - half, 0:16] = packed(vreg, 4, edge)
-        for j in range(ROWS):
-            total = jnp.zeros((8, TILE), jnp.float32)
-            for q in range(GROUPS):
-                rows = pl.ds(8 * q, 8)
-                density = THERMAL * x[T, j + 1, rows, cut] - HALINE * x[S, j + 1, rows, cut]
-                total = total + jnp.where(wet(j, q), density, 0.0)
-            surface[BUOYANT, ROWS + j : ROWS + j + 1, cut] = (LEVELS**-0.5) * jnp.sum(total, 0, keepdims=True)
-        kept = (where >= TILE - 8) if half else (where < 8)
-        lon_out[1 - half, 16:24] = sum(
-            turn(jnp.where(kept, surface[f, plane, cut], 0.0), 16 * f, 1)
-            for f in range(FIELDS)
-        )
-
-    wait_half(1)
-    pack_half(1)
+        def surface_part():
+            for j in range(ROWS):
+                total = jnp.zeros((8, TILE), jnp.float32)
+                for q in range(GROUPS):
+                    rows = pl.ds(8 * q, 8)
+                    density = THERMAL * x[T, j + 1, rows, cut] - HALINE * x[S, j + 1, rows, cut]
+                    total = total + jnp.where(wet(j, q), density, 0.0)
+                surface[BUOYANT, ROWS + j : ROWS + j + 1, cut] = (LEVELS**-0.5) * jnp.sum(total, 0, keepdims=True)
+            kept = (where >= TILE - 8) if half else (where < 8)
+            lon_out[1 - half, 16:24] = sum(
+                turn(jnp.where(kept, surface[f, plane, cut], 0.0), 16 * f, 1)
+                for f in range(FIELDS)
+            )
+
+        def tracer_part():
+            lon_out[1 - half, 0:16] = packed(vreg, 4, edge, range(ROWS))
+
+        return surface_part, tracer_part
+
+    surface_part, tracer_part = pack_half(1)
+    wait_half(1, T, 2, 4)
+    for c in surface_loads:
+        c.wait()
+    surface_part()
+
+    @pl.when(late)
+    def _():
+        pl.semaphore_wait(barrier, expected)
+
+    send(NE)
+    send(SE)
+    wait_half(1, U, 1, 5)
+    tracer_part()
+    send(E)
     for way in (E, NE, SE):
-        send(way)
-    wait_half(0)
-    pack_half(0)
+        signal(seam_sem, way, late)
+    signal(ready_sem, N, both(late, last_in_pair_n))
+    signal(ready_sem, S_, both(late, last_in_pair_s))
+    send_depth(usual)
+    wait_half(0, U, 3, 6)
+    for part in pack_half(0):
+        part()
     send(W, jnp.logical_not(early))
     middle = jnp.logical_and(usual, jnp.logical_not(early))
     send(NW, middle)
     send(SW, middle)
-    send(N, usual)
-    send(S_, usual)
-
-    @pl.when(late)
+
+    lasts = jnp.where(north_first, 0, count_n) + jnp.where(south_first, 0, count_s)
+
+    @pl.when(both(late, lasts > 0))
     def _():
-        pl.semaphore_wait(ready_sem, 2 * sides)
+        pl.semaphore_wait(ready_sem, 2 * lasts)
 
     send_rows(late)
-    for way in (NW, SW, N, S_):
-        send(way, late)
+    send_depth(late)
+    send(NW, late)
+    send(SW, late)
 
     for c in weights:
         c.wait()
     w1_t[...] = w1_in[...].astype(jnp.float32).T.astype(jnp.bfloat16)
     all_v = x.at[V, pl.ds(1, ROWS)]
-    local(all_v, all_v, load_sem.at[6]).wait()
+    local(all_v, all_v, load_sem.at[7]).wait()
 
     def row(j):
         level = levels_of(COLS)
@@ -331,47 +377,53 @@
         out_s[j] = settle(saline, kappa)
 
     pl.loop(1, ROWS - 1)(row)
-
-    @pl.when(early)
-    def _():
-        pl.semaphore_wait(seam_sem, 1 + sides)
-
-    signal(ready_sem, NW, early)
-    signal(ready_sem, SW, early)
-    for way in (W, NW, SW):
-        send(way, early)
-
-    for way in (N, S_):
-
-        @pl.when(there[way])
-        def _(way=way):
-            k = way - N
-            rows = x.at[pl.ds(T, 3), ROWS + 1 if way == N else 0]
-            local(rows, rows, row_recv.at[k]).wait()
-            message(opposite[way]).wait_recv()
-
-    deep[0] = jnp.broadcast_to(surface[DEPTH, ROWS - 1 : ROWS], (8, COLS))
-    deep[ROWS + 1] = jnp.broadcast_to(surface[DEPTH, 2 * ROWS : 2 * ROWS + 1], (8, COLS))
-
-    @pl.loop(0, 2)
-    def _(i):
-        row(i * (ROWS - 1))
-
-    def side_pack(half):
+    send(N)
+    send(S_)
+
+    def side_pack(half, rows):
         cut = pl.ds(half * TILE, TILE)
         return packed(
             lambda a, j, q: side[a, j, pl.ds(8 * q, 8), cut],
             2,
             TILE - 1 if half else 0,
+            rows,
         )
 
-    part_east, part_west = side_pack(1), side_pack(0)
-
-    for way in (E, W, NE, SE, NW, SW):
-
-        @pl.when(there[way])
-        def _(way=way):
-            message(opposite[way]).wait_recv()
+    inside = range(1, ROWS - 1)
+    part_east, part_west = side_pack(1, inside), side_pack(0, inside)
+
+    near_north = lax.rem(lat, 2) == 0
+
+    def outer(north):
+        for way in (N, S_):
+
+            @pl.when(jnp.logical_and(there[way], north if way == N else jnp.logical_not(north)))
+            def _(way=way):
+                k = way - N
+                rows = x.at[pl.ds(T, 3), ROWS + 1 if way == N else 0]
+                local(rows, rows, row_recv.at[k]).wait()
+                depth_message(opposite[way]).wait_recv()
+
+        edge = jnp.where(north, ROWS - 1, 0)
+        beyond = jnp.where(north, 2 * ROWS, ROWS - 1)
+        deep[jnp.where(north, ROWS + 1, 0)] = jnp.broadcast_to(surface[DEPTH, pl.ds(beyond, 1)], (8, COLS))
+        row(edge)
+        return side_pack(1, [edge]), side_pack(0, [edge])
+
+    near_east, near_west = outer(near_north)
+    far_east, far_west = outer(jnp.logical_not(near_north))
+    part_east = part_east + near_east + far_east
+    part_west = part_west + near_west + far_west
+
+    @pl.when(early)
+    def _():
+        pl.semaphore_wait(seam_sem, 1 + sides)
+
+    for way in (W, NW, SW):
+        send(way, early)
+
+    for way in (E, W):
+        message(opposite[way]).wait_recv()
 
     own_east, own_west = lon_out[0, 0:16], lon_out[1, 0:16]
     from_east, from_west = lon_in[0, 0:16], lon_in[1, 0:16]
@@ -393,6 +445,12 @@
             out[j, :, 0:TILE] = jnp.where(lane == 0, turn(new, -j, 1), out[j, :, 0:TILE])
             out[j, :, TILE:] = jnp.where(lane == TILE - 1, turn(new, TILE - 1 - 8 - j, 1), out[j, :, TILE:])
 
+    for way in (N, S_, NE, SE, NW, SW):
+
+        @pl.when(there[way])
+        def _(way=way):
+            message(opposite[way]).wait_recv()
+
     third = jnp.concatenate(
         [
             corner_in[1] + corner_in[3],
@@ -407,7 +465,7 @@
         jnp.concatenate([surface[f], jnp.where(around, turn(third, -16 * f, 1), 0.0)], 1)
         for f in range(FIELDS)
     ]
-    h, e, n, d, b = field
+    h, e, n, b, d = field
     land = d <= 0.0
     column = d * (1.0 / LEVELS)
 
@@ -431,6 +489,7 @@
         def _(way=way):
             for c in row_copies(way):
                 c.wait_send()
+            depth_message(way).wait_send()
 
     for way in range(8):
 
@@ -480,8 +539,10 @@
                 pltpu.VMEM((2, 24, TILE), f32),
                 pltpu.VMEM((2, 24, TILE), f32),
                 pltpu.VMEM((4, 8, TILE), f32),
-                dma((9,)),
+                dma((10,)),
                 dma((6,)),
+                dma((2,)),
+                dma((2,)),
                 dma((2,)),
                 dma((8,)),
                 dma((8,)),

time: 20.3 us -> 19.4 us (0.956)
  the two profiles are of different devices: /device:TPU:491 before, /device:TPU:1 now
where the time goes in v2:
time: 19.4 us; the launch traced here: 19.1 us
  Pallas kernels  18.5 us (95%)
  between operations  0.64 us (3%)
    pallas_call x1, Pallas kernels, local(): pl.pallas_call(functools.partial(exchange, nlon, nlat), out_shape=(rows,...  17.4 us
    pallas_call x1, Pallas kernels, local(): pl.pallas_call(deliver, out_shape=(block, block, plane, plane, plane), in...  1.13 us

profile of v2, /device:TPU:1, one launch (start us, length us, event | category | flops | bytes accessed | tf_op | source)
XLA Modules:
  0.0 19.1 jit_solution(17414875355466663352)
XLA Ops:
  0.6 17.4 %shard_map.137 = (f32[8,64,256]{2,1,0:T(8,128)S(1)}, f32[8,64,256]{2,1,0:T(8,128)S(1)}, f32[3,8,256]{2,1,0:T(8,128)S(1)}) custom-call(f32[64,8,256]{2,1,0:T(8,128)} %t.1, f32[64,8,256]{2,1,0:T(8,128)} %s.1, f32[64,8,256]{2,1,0:T(8,128)} %u.1, f32[64,8,256]{2,1,0:T(8,128)} %v.1, s32[8,256]{1,0:T(8,128)} %depth.1, f32[8,256]{1,0:T(8,128)} %height.1, ...), custom_call_target="tpu_custom_call" | custom-call | tf_op jit(solution)/shard_map/pallas_call | solution.py:524
  18.0 1.1 %shard_map.138 = (f32[64,8,256]{2,1,0:T(8,128)}, f32[64,8,256]{2,1,0:T(8,128)}, f32[8,256]{1,0:T(8,128)}, f32[8,256]{1,0:T(8,128)}, f32[8,256]{1,0:T(8,128)}) custom-call(f32[8,64,256]{2,1,0:T(8,128)S(1)} %get-tuple-element.8.t, f32[8,64,256]{2,1,0:T(8,128)S(1)} %get-tuple-element.9.s, f32[3,8,256]{2,1,0:T(8,128)S(1)} %get-tuple-element.10.surface), custom_call_target="tpu_custom_call" | custom-call | tf_op jit(solution)/shard_map/pallas_call | solution.py:556

commit v3 on v2

--- a/solution.py
+++ b/solution.py
@@ -103,7 +103,7 @@
     t, s, u, v, depth, height, east, north, w1, w2,
     out_t, out_s, out_surface,
     x, side, surface, depth_int, w1_in, w1_t, w2_t, deep, deep_east, lon_out, lon_in, corner_in,
-    load_sem, row_send, row_recv, depth_send, depth_recv, send_sem, recv_sem, seam_sem, ready_sem,
+    load_sem, row_send, row_recv, depth_send, depth_recv, send_sem, recv_sem, seam_sem, ready_sem, east_sem,
 ):
     lon, lat = lax.axis_index("lon"), lax.axis_index("lat")
     z = lax.rem(lon, PERIOD)
@@ -146,45 +146,28 @@
         whole = x.at[pl.ds(k, count), pl.ds(1, ROWS), :, pl.ds(half * TILE, TILE)]
         local(whole, whole, load_sem.at[sem]).wait()
 
-    depth_load.start()
+    for c in (depth_load, *surface_loads):
+        c.start()
     load_half(1, ((T, t), (S, s)), 4)
-    for c in surface_loads:
-        c.start()
     load_half(1, ((U, u),), 5)
 
     barrier = pltpu.get_barrier_semaphore()
-    signal(barrier, W)
-    signal(barrier, NW)
-    signal(barrier, SW)
     usual = jnp.logical_not(late)
     both = jnp.logical_and
-    place, half_one = lax.rem(lat, 4), lon < nlon // 2
-    north_first = jnp.where(place == 3, half_one, place != 1)
-    south_first = jnp.where(place == 0, jnp.logical_not(half_one), place == 2)
-    last_in_pair_n, last_in_pair_s = north_first, south_first
-    signal(barrier, E, usual)
-    signal(barrier, N, jnp.logical_or(usual, jnp.logical_not(last_in_pair_n)))
-    signal(barrier, S_, jnp.logical_or(usual, jnp.logical_not(last_in_pair_s)))
-    signal(barrier, NE, both(usual, jnp.logical_not(both(before, last_in_pair_n))))
-    signal(barrier, SE, both(usual, jnp.logical_not(both(before, last_in_pair_s))))
-
-    load_half(0, ((T, t), (S, s), (U, u)), 6)
-    for j in range(ROWS):
-        local(v.at[:, j, :], x.at[V, j + 1], load_sem.at[7]).start()
-    weights = [local(w1, w1_in, load_sem.at[8]), local(w2, w2_t, load_sem.at[9])]
-    for c in weights:
-        c.start()
-
-    count_n, count_s = has_n.astype(jnp.int32), has_s.astype(jnp.int32)
-    firsts = jnp.where(north_first, count_n, 0) + jnp.where(south_first, count_s, 0)
-    expected = jnp.where(early, 1 + 2 * sides, jnp.where(late, 2 + sides + 2 * firsts, 2 + 3 * sides))
-
-    @pl.when(usual)
-    def _():
-        pl.semaphore_wait(barrier, expected)
-
-    signal(ready_sem, NE, both(before, last_in_pair_n))
-    signal(ready_sem, SE, both(before, last_in_pair_s))
+    inner = both(usual, jnp.logical_not(before))
+    for way in (E, NE, SE):
+        signal(barrier, way, inner)
+    for way in (W, NW, SW):
+        signal(barrier, way, jnp.logical_or(early, late))
+    signal(barrier, N, usual)
+    signal(barrier, S_, usual)
+    expected = jnp.where(early, sides, jnp.where(late, 1 + sides, jnp.where(before, 2 + 3 * sides, 1 + 2 * sides)))
+    pl.semaphore_wait(barrier, expected)
+    signal(ready_sem, E, before)
+    for way in (E, NE, SE):
+        signal(seam_sem, way, late)
+    for way in (W, NW, SW):
+        signal(east_sem, way, jnp.logical_not(jnp.logical_or(early, late)))
 
     remote = pltpu.make_async_remote_copy
 
@@ -303,39 +286,34 @@
     for c in surface_loads:
         c.wait()
     surface_part()
-
-    @pl.when(late)
-    def _():
-        pl.semaphore_wait(barrier, expected)
-
-    send(NE)
-    send(SE)
+    at_once = jnp.logical_not(inner)
+    send(NE, at_once)
+    send(SE, at_once)
     wait_half(1, U, 1, 5)
     tracer_part()
-    send(E)
-    for way in (E, NE, SE):
-        signal(seam_sem, way, late)
-    signal(ready_sem, N, both(late, last_in_pair_n))
-    signal(ready_sem, S_, both(late, last_in_pair_s))
+    send(E, at_once)
+    load_half(0, ((T, t), (S, s), (U, u)), 6)
+    for j in range(ROWS):
+        local(v.at[:, j, :], x.at[V, j + 1], load_sem.at[7]).start()
+    weights = [local(w1, w1_in, load_sem.at[8]), local(w2, w2_t, load_sem.at[9])]
+    for c in weights:
+        c.start()
     send_depth(usual)
     wait_half(0, U, 3, 6)
     for part in pack_half(0):
         part()
-    send(W, jnp.logical_not(early))
     middle = jnp.logical_and(usual, jnp.logical_not(early))
-    send(NW, middle)
-    send(SW, middle)
-
-    lasts = jnp.where(north_first, 0, count_n) + jnp.where(south_first, 0, count_s)
-
-    @pl.when(both(late, lasts > 0))
+    for way in (W, NW, SW):
+        send(way, middle)
+
+    @pl.when(late)
     def _():
-        pl.semaphore_wait(ready_sem, 2 * lasts)
+        pl.semaphore_wait(ready_sem, 1)
 
     send_rows(late)
     send_depth(late)
-    send(NW, late)
-    send(SW, late)
+    for way in (W, NW, SW):
+        send(way, late)
 
     for c in weights:
         c.wait()
@@ -377,6 +355,13 @@
         out_s[j] = settle(saline, kappa)
 
     pl.loop(1, ROWS - 1)(row)
+
+    @pl.when(inner)
+    def _():
+        pl.semaphore_wait(east_sem, 1 + sides)
+
+    for way in (E, NE, SE):
+        send(way, inner)
     send(N)
     send(S_)
 
@@ -466,20 +451,38 @@
         for f in range(FIELDS)
     ]
     h, e, n, b, d = field
+    def ahead_behind(a, axis, by):
+        return turn(a, -by, axis), turn(a, by, axis)
+
+    def current(flow, axis):
+        flows, depths = ahead_behind(flow, axis, 1), ahead_behind(d, axis, 1)
+        after, before_ = ahead_behind(b, axis, 2)
+        forces = -BUOYANCY * (after - b), -BUOYANCY * (b - before_)
+        return [
+            (f, g, p <= 0.0, p * (1.0 / LEVELS)) for f, g, p in zip(flows, forces, depths)
+        ]
+
     land = d <= 0.0
-    column = d * (1.0 / LEVELS)
-
-    def eastward(a):
-        return turn(a, -1, 1) - turn(a, 1, 1)
-
-    def northward(a):
-        return turn(a, -1, 0) - turn(a, 1, 0)
-
-    east_force, north_force = -BUOYANCY * eastward(b), -BUOYANCY * northward(b)
-    for _ in range(SUBSTEPS):
-        e = jnp.where(land, 0.0, e - GRAVITY * eastward(h) + east_force)
-        n = jnp.where(land, 0.0, n - GRAVITY * northward(h) + north_force)
-        h = jnp.where(land, 0.0, h - SPREADING * (eastward(column * e) + northward(column * n)))
+    state = {1: current(e, 1), 0: current(n, 0)}
+    for step in range(SUBSTEPS):
+        carried = 0.0
+        if step == SUBSTEPS - 1:
+            (e, force, _, _), (n, force_n, _, _) = state[1][0], state[0][0]
+            e, n = turn(e, 1, 1), turn(n, 1, 0)
+            rises = [ahead_behind(h, axis, 1) for axis in (1, 0)]
+            e = e - GRAVITY * (rises[0][0] - rises[0][1]) + turn(force, 1, 1)
+            n = n - GRAVITY * (rises[1][0] - rises[1][1]) + turn(force_n, 1, 0)
+            e, n = jnp.where(land, 0.0, e), jnp.where(land, 0.0, n)
+        for axis in (1, 0):
+            after, before_ = ahead_behind(h, axis, 2)
+            slopes = after - h, h - before_
+            state[axis] = [
+                (jnp.where(dry, 0.0, f - GRAVITY * slope + g), g, dry, c)
+                for (f, g, dry, c), slope in zip(state[axis], slopes)
+            ]
+            (ahead, _, _, c_ahead), (behind, _, _, c_behind) = state[axis]
+            carried = carried + (c_ahead * ahead - c_behind * behind)
+        h = jnp.where(land, 0.0, h - SPREADING * carried)
     for k, a in enumerate((h, e, n)):
         out_surface[k] = a[ROWS : 2 * ROWS, 0:COLS]
 
@@ -548,6 +551,7 @@
                 dma((8,)),
                 pltpu.SemaphoreType.REGULAR,
                 pltpu.SemaphoreType.REGULAR,
+                pltpu.SemaphoreType.REGULAR,
             ],
             compiler_params=pltpu.CompilerParams(
                 collective_id=0, has_side_effects=True, vmem_limit_bytes=LIMIT

time: 19.4 us -> 19 us (0.979)
  Pallas kernels: 18.5 us -> 18 us
    pallas_call x1, Pallas kernels: 17.4 us -> 16.9 us  [local(): pl.pallas_call(functools.partial(exchange, nlon, nlat), out_shape=(rows,...]
where the time goes in v3:
time: 19 us; the launch traced here: 18.7 us
  Pallas kernels  18 us (95%)
  between operations  0.64 us (3%)
    pallas_call x1, Pallas kernels, local(): pl.pallas_call(functools.partial(exchange, nlon, nlat), out_shape=(rows,...  16.9 us
    pallas_call x1, Pallas kernels, local(): pl.pallas_call(deliver, out_shape=(block, block, plane, plane, plane), in...  1.13 us

profile of v3, /device:TPU:1, one launch (start us, length us, event | category | flops | bytes accessed | tf_op | source)
XLA Modules:
  0.0 18.7 jit_solution(7897547551045779620)
XLA Ops:
  0.6 16.9 %shard_map.137 = (f32[8,64,256]{2,1,0:T(8,128)S(1)}, f32[8,64,256]{2,1,0:T(8,128)S(1)}, f32[3,8,256]{2,1,0:T(8,128)S(1)}) custom-call(f32[64,8,256]{2,1,0:T(8,128)} %t.1, f32[64,8,256]{2,1,0:T(8,128)} %s.1, f32[64,8,256]{2,1,0:T(8,128)} %u.1, f32[64,8,256]{2,1,0:T(8,128)} %v.1, s32[8,256]{1,0:T(8,128)} %depth.1, f32[8,256]{1,0:T(8,128)} %height.1, ...), custom_call_target="tpu_custom_call" | custom-call | tf_op jit(solution)/shard_map/pallas_call | solution.py:527
  17.5 1.1 %shard_map.138 = (f32[64,8,256]{2,1,0:T(8,128)}, f32[64,8,256]{2,1,0:T(8,128)}, f32[8,256]{1,0:T(8,128)}, f32[8,256]{1,0:T(8,128)}, f32[8,256]{1,0:T(8,128)}) custom-call(f32[8,64,256]{2,1,0:T(8,128)S(1)} %get-tuple-element.8.t, f32[8,64,256]{2,1,0:T(8,128)S(1)} %get-tuple-element.9.s, f32[3,8,256]{2,1,0:T(8,128)S(1)} %get-tuple-element.10.surface), custom_call_target="tpu_custom_call" | custom-call | tf_op jit(solution)/shard_map/pallas_call | solution.py:560

commit v4 on v3

--- a/solution.py
+++ b/solution.py
@@ -25,7 +25,7 @@
 U, T, S, V = range(4)
 HEIGHT, EAST, NORTH, BUOYANT, DEPTH = range(5)
 FIELDS = 5
-E, W, N, S_, NE, SE, NW, SW = range(8)
+E, W, N, S_, NE, SE, NW, SW, E_SURFACE, W_SURFACE = range(10)
 
 
 def turn(x, shift, axis):
@@ -103,7 +103,7 @@
     t, s, u, v, depth, height, east, north, w1, w2,
     out_t, out_s, out_surface,
     x, side, surface, depth_int, w1_in, w1_t, w2_t, deep, deep_east, lon_out, lon_in, corner_in,
-    load_sem, row_send, row_recv, depth_send, depth_recv, send_sem, recv_sem, seam_sem, ready_sem, east_sem,
+    load_sem, row_send, row_recv, depth_send, depth_recv, send_sem, recv_sem, seam_sem, seam_corner_sem, ready_sem, east_sem, origin_sem,
 ):
     lon, lat = lax.axis_index("lon"), lax.axis_index("lat")
     z = lax.rem(lon, PERIOD)
@@ -120,8 +120,10 @@
         SE: {"lon": to_east, "lat": lat - 1},
         NW: {"lon": to_west, "lat": lat + 1},
         SW: {"lon": to_west, "lat": lat - 1},
+        E_SURFACE: {"lon": to_east},
+        W_SURFACE: {"lon": to_west},
     }
-    there = {E: True, W: True, N: has_n, NE: has_n, NW: has_n, S_: has_s, SE: has_s, SW: has_s}
+    there = {E: True, W: True, N: has_n, NE: has_n, NW: has_n, S_: has_s, SE: has_s, SW: has_s, E_SURFACE: True, W_SURFACE: True}
 
     def signal(sem, way, also=True):
         @pl.when(jnp.logical_and(there[way], also))
@@ -146,28 +148,53 @@
         whole = x.at[pl.ds(k, count), pl.ds(1, ROWS), :, pl.ds(half * TILE, TILE)]
         local(whole, whole, load_sem.at[sem]).wait()
 
+    barrier = pltpu.get_barrier_semaphore()
+
+    @pl.when(late)
+    def _():
+        pl.semaphore_wait(barrier, 1 + sides)
+
+    signal(seam_corner_sem, SE, late)
+    signal(seam_corner_sem, NE, late)
+    signal(seam_sem, E, late)
+
     for c in (depth_load, *surface_loads):
         c.start()
     load_half(1, ((T, t), (S, s)), 4)
     load_half(1, ((U, u),), 5)
 
-    barrier = pltpu.get_barrier_semaphore()
     usual = jnp.logical_not(late)
     both = jnp.logical_and
     inner = both(usual, jnp.logical_not(before))
-    for way in (E, NE, SE):
-        signal(barrier, way, inner)
+    origin = both(lon == 0, lat == 0)
+    not_origin = jnp.logical_not(origin)
+    at_n, at_e, at_ne = both(lon == 0, lat == 1), both(lon == 1, lat == 0), both(lon == 1, lat == 1)
+    held = {S_: at_n, W: at_e, W_SURFACE: at_e, SW: at_ne}
+
+    def free(way, also):
+        return both(also, jnp.logical_not(held[way])) if way in held else also
+
+    for way, also in ((E, inner), (NE, inner), (N, usual)):
+        signal(barrier, way, both(also, not_origin))
+    signal(barrier, SE, inner)
+    signal(barrier, S_, usual)
+    edge_of_z = jnp.logical_or(early, late)
+    signal(barrier, W, jnp.logical_or(edge_of_z, at_e))
+    signal(barrier, NW, edge_of_z)
+    signal(barrier, SW, jnp.logical_or(edge_of_z, at_ne))
+    expected = jnp.where(early, sides, jnp.where(before, 2 + 3 * sides, 1 + 2 * sides))
+    beside_origin = jnp.logical_or(at_n, jnp.logical_or(at_e, at_ne))
+    expected = expected + jnp.where(origin, 2, 0) - jnp.where(beside_origin, 1, 0)
+
+    @pl.when(usual)
+    def _():
+        pl.semaphore_wait(barrier, expected)
+
+    for way in (N, E, NE):
+        signal(origin_sem, way, origin)
+    signal(ready_sem, E, before)
     for way in (W, NW, SW):
-        signal(barrier, way, jnp.logical_or(early, late))
-    signal(barrier, N, usual)
-    signal(barrier, S_, usual)
-    expected = jnp.where(early, sides, jnp.where(late, 1 + sides, jnp.where(before, 2 + 3 * sides, 1 + 2 * sides)))
-    pl.semaphore_wait(barrier, expected)
-    signal(ready_sem, E, before)
-    for way in (E, NE, SE):
-        signal(seam_sem, way, late)
-    for way in (W, NW, SW):
-        signal(east_sem, way, jnp.logical_not(jnp.logical_or(early, late)))
+        signal(east_sem, way, free(way, jnp.logical_not(edge_of_z)))
 
     remote = pltpu.make_async_remote_copy
 
@@ -180,15 +207,17 @@
             for i, (a, f) in enumerate(((T, t), (S, s), (V, v)))
         ]
 
-    opposite = {E: W, W: E, N: S_, S_: N, NE: SW, SW: NE, NW: SE, SE: NW}
-    lon_slot = {E: 0, W: 1}
+    opposite = {E: W, W: E, N: S_, S_: N, NE: SW, SW: NE, NW: SE, SE: NW, E_SURFACE: W_SURFACE, W_SURFACE: E_SURFACE}
+    lon_slot = {E: 0, W: 1, E_SURFACE: 0, W_SURFACE: 1}
+    eastward, westward = (E, NE, SE, E_SURFACE), (W, NW, SW, W_SURFACE)
     corner_slot = {NE: 0, SE: 1, NW: 2, SW: 3}
     surface_rows = {N: pl.ds(2 * ROWS, ROWS), S_: pl.ds(0, ROWS)}
     tail = pl.ds(16, 8)
 
     def message(way):
         if way in lon_slot:
-            src, dst = lon_out.at[lon_slot[way]], lon_in.at[lon_slot[opposite[way]]]
+            part = pl.ds(0, 16) if way in (E, W) else tail
+            src, dst = lon_out.at[lon_slot[way], part], lon_in.at[lon_slot[opposite[way]], part]
         elif way in corner_slot:
             src = lon_out.at[0 if way in (NE, SE) else 1, tail]
             dst = corner_in.at[corner_slot[opposite[way]]]
@@ -206,19 +235,19 @@
     def send_depth(also):
         for way in (N, S_):
 
-            @pl.when(jnp.logical_and(there[way], also))
+            @pl.when(jnp.logical_and(there[way], free(way, also)))
             def _(way=way):
                 depth_message(way).start()
 
-    def send(way, also=True):
-        @pl.when(jnp.logical_and(there[way], also))
+    def send(way, also):
+        @pl.when(jnp.logical_and(there[way], free(way, also)))
         def _():
             message(way).start()
 
     def send_rows(also):
         for way in (N, S_):
 
-            @pl.when(jnp.logical_and(there[way], also))
+            @pl.when(jnp.logical_and(there[way], free(way, also)))
             def _(way=way):
                 for c in row_copies(way):
                     c.start()
@@ -285,13 +314,21 @@
     wait_half(1, T, 2, 4)
     for c in surface_loads:
         c.wait()
-    surface_part()
     at_once = jnp.logical_not(inner)
-    send(NE, at_once)
-    send(SE, at_once)
+    place = lax.rem(lat, 4)
+
+    def surface_first(also):
+        @pl.when(also)
+        def _():
+            surface_part()
+            for way in (NE, SE, E_SURFACE):
+                send(way, at_once)
+
+    surface_first(place == 2)
     wait_half(1, U, 1, 5)
     tracer_part()
     send(E, at_once)
+    surface_first(place != 2)
     load_half(0, ((T, t), (S, s), (U, u)), 6)
     for j in range(ROWS):
         local(v.at[:, j, :], x.at[V, j + 1], load_sem.at[7]).start()
@@ -303,8 +340,10 @@
     for part in pack_half(0):
         part()
     middle = jnp.logical_and(usual, jnp.logical_not(early))
-    for way in (W, NW, SW):
+    for way in westward:
         send(way, middle)
+    near_north = lax.rem(lat, 2) == 0
+    far_north = jnp.logical_not(near_north)
 
     @pl.when(late)
     def _():
@@ -312,8 +351,20 @@
 
     send_rows(late)
     send_depth(late)
-    for way in (W, NW, SW):
+    for way in westward:
         send(way, late)
+    send(N, near_north)
+    send(S_, far_north)
+
+    def send_east(also):
+        @pl.when(both(also, not_origin))
+        def _():
+            pl.semaphore_wait(east_sem, 1 + sides)
+
+        for way in eastward:
+            send(way, also)
+
+    send_east(early)
 
     for c in weights:
         c.wait()
@@ -356,14 +407,29 @@
 
     pl.loop(1, ROWS - 1)(row)
 
-    @pl.when(inner)
-    def _():
-        pl.semaphore_wait(east_sem, 1 + sides)
-
-    for way in (E, NE, SE):
-        send(way, inner)
-    send(N)
-    send(S_)
+    send_east(both(inner, jnp.logical_not(early)))
+    send(N, far_north)
+    send(S_, near_north)
+
+    @pl.when(beside_origin)
+    def _():
+        pl.semaphore_wait(origin_sem, 1)
+
+    @pl.when(at_n)
+    def _():
+        for c in row_copies(S_):
+            c.start()
+        depth_message(S_).start()
+        message(S_).start()
+
+    @pl.when(at_e)
+    def _():
+        message(W).start()
+        message(W_SURFACE).start()
+
+    @pl.when(at_ne)
+    def _():
+        message(SW).start()
 
     def side_pack(half, rows):
         cut = pl.ds(half * TILE, TILE)
@@ -377,7 +443,6 @@
     inside = range(1, ROWS - 1)
     part_east, part_west = side_pack(1, inside), side_pack(0, inside)
 
-    near_north = lax.rem(lat, 2) == 0
 
     def outer(north):
         for way in (N, S_):
@@ -396,16 +461,23 @@
         return side_pack(1, [edge]), side_pack(0, [edge])
 
     near_east, near_west = outer(near_north)
-    far_east, far_west = outer(jnp.logical_not(near_north))
+    far_east, far_west = outer(far_north)
     part_east = part_east + near_east + far_east
     part_west = part_west + near_west + far_west
 
     @pl.when(early)
     def _():
-        pl.semaphore_wait(seam_sem, 1 + sides)
-
-    for way in (W, NW, SW):
-        send(way, early)
+        pl.semaphore_wait(seam_sem, 1)
+
+    send(W, early)
+    send(W_SURFACE, early)
+
+    @pl.when(early)
+    def _():
+        pl.semaphore_wait(seam_corner_sem, sides)
+
+    send(NW, early)
+    send(SW, early)
 
     for way in (E, W):
         message(opposite[way]).wait_recv()
@@ -430,7 +502,21 @@
             out[j, :, 0:TILE] = jnp.where(lane == 0, turn(new, -j, 1), out[j, :, 0:TILE])
             out[j, :, TILE:] = jnp.where(lane == TILE - 1, turn(new, TILE - 1 - 8 - j, 1), out[j, :, TILE:])
 
-    for way in (N, S_, NE, SE, NW, SW):
+    for way in (N, S_):
+
+        @pl.when(there[way])
+        def _(way=way):
+            for c in row_copies(way):
+                c.wait_send()
+            depth_message(way).wait_send()
+
+    for way in range(10):
+
+        @pl.when(there[way])
+        def _(way=way):
+            message(way).wait_send()
+
+    for way in (N, S_, NE, SE, NW, SW, E_SURFACE, W_SURFACE):
 
         @pl.when(there[way])
         def _(way=way):
@@ -485,20 +571,6 @@
         h = jnp.where(land, 0.0, h - SPREADING * carried)
     for k, a in enumerate((h, e, n)):
         out_surface[k] = a[ROWS : 2 * ROWS, 0:COLS]
-
-    for way in (N, S_):
-
-        @pl.when(there[way])
-        def _(way=way):
-            for c in row_copies(way):
-                c.wait_send()
-            depth_message(way).wait_send()
-
-    for way in range(8):
-
-        @pl.when(there[way])
-        def _(way=way):
-            message(way).wait_send()
 
 
 def deliver(t, s, surface, out_t, out_s, height, east, north, sem):
@@ -547,8 +619,10 @@
                 dma((2,)),
                 dma((2,)),
                 dma((2,)),
-                dma((8,)),
-                dma((8,)),
+                dma((10,)),
+                dma((10,)),
+                pltpu.SemaphoreType.REGULAR,
+                pltpu.SemaphoreType.REGULAR,
                 pltpu.SemaphoreType.REGULAR,
                 pltpu.SemaphoreType.REGULAR,
                 pltpu.SemaphoreType.REGULAR,

time: 19 us -> 19 us (level)
  no operation moved by 1% of the time
where the time goes in v4:
time: 19 us; the launch traced here: 18.7 us
  Pallas kernels  18.1 us (95%)
  between operations  0.64 us (3%)
    pallas_call x1, Pallas kernels, local(): pl.pallas_call(functools.partial(exchange, nlon, nlat), out_shape=(rows,...  17 us
    pallas_call x1, Pallas kernels, local(): pl.pallas_call(deliver, out_shape=(block, block, plane, plane, plane), in...  1.13 us

profile of v4, /device:TPU:1, one launch (start us, length us, event | category | flops | bytes accessed | tf_op | source)
XLA Modules:
  0.0 18.7 jit_solution(12510853069079305458)
XLA Ops:
  0.6 17.0 %shard_map.137 = (f32[8,64,256]{2,1,0:T(8,128)S(1)}, f32[8,64,256]{2,1,0:T(8,128)S(1)}, f32[3,8,256]{2,1,0:T(8,128)S(1)}) custom-call(f32[64,8,256]{2,1,0:T(8,128)} %t.1, f32[64,8,256]{2,1,0:T(8,128)} %s.1, f32[64,8,256]{2,1,0:T(8,128)} %u.1, f32[64,8,256]{2,1,0:T(8,128)} %v.1, s32[8,256]{1,0:T(8,128)} %depth.1, f32[8,256]{1,0:T(8,128)} %height.1, ...), custom_call_target="tpu_custom_call" | custom-call | tf_op jit(solution)/shard_map/pallas_call | solution.py:599
  17.6 1.1 %shard_map.138 = (f32[64,8,256]{2,1,0:T(8,128)}, f32[64,8,256]{2,1,0:T(8,128)}, f32[8,256]{1,0:T(8,128)}, f32[8,256]{1,0:T(8,128)}, f32[8,256]{1,0:T(8,128)}) custom-call(f32[8,64,256]{2,1,0:T(8,128)S(1)} %get-tuple-element.8.t, f32[8,64,256]{2,1,0:T(8,128)S(1)} %get-tuple-element.9.s, f32[3,8,256]{2,1,0:T(8,128)S(1)} %get-tuple-element.10.surface), custom_call_target="tpu_custom_call" | custom-call | tf_op jit(solution)/shard_map/pallas_call | solution.py:634

commit v5 on v4

--- a/solution.py
+++ b/solution.py
@@ -158,9 +158,9 @@
     signal(seam_corner_sem, NE, late)
     signal(seam_sem, E, late)
 
+    load_half(1, ((T, t), (S, s)), 4)
     for c in (depth_load, *surface_loads):
         c.start()
-    load_half(1, ((T, t), (S, s)), 4)
     load_half(1, ((U, u),), 5)
 
     usual = jnp.logical_not(late)
@@ -321,7 +321,7 @@
         @pl.when(also)
         def _():
             surface_part()
-            for way in (NE, SE, E_SURFACE):
+            for way in (SE, NE, E_SURFACE):
                 send(way, at_once)
 
     surface_first(place == 2)

time: 19 us -> 19 us (level)
  no operation moved by 1% of the time
where the time goes in v5:
time: 19 us; the launch traced here: 18.7 us
  Pallas kernels  18 us (95%)
  between operations  0.64 us (3%)
    pallas_call x1, Pallas kernels, local(): pl.pallas_call(functools.partial(exchange, nlon, nlat), out_shape=(rows,...  16.9 us
    pallas_call x1, Pallas kernels, local(): pl.pallas_call(deliver, out_shape=(block, block, plane, plane, plane), in...  1.13 us

profile of v5, /device:TPU:1, one launch (start us, length us, event | category | flops | bytes accessed | tf_op | source)
XLA Modules:
  0.0 18.7 jit_solution(14772030248932922044)
XLA Ops:
  0.6 16.9 %shard_map.137 = (f32[8,64,256]{2,1,0:T(8,128)S(1)}, f32[8,64,256]{2,1,0:T(8,128)S(1)}, f32[3,8,256]{2,1,0:T(8,128)S(1)}) custom-call(f32[64,8,256]{2,1,0:T(8,128)} %t.1, f32[64,8,256]{2,1,0:T(8,128)} %s.1, f32[64,8,256]{2,1,0:T(8,128)} %u.1, f32[64,8,256]{2,1,0:T(8,128)} %v.1, s32[8,256]{1,0:T(8,128)} %depth.1, f32[8,256]{1,0:T(8,128)} %height.1, ...), custom_call_target="tpu_custom_call" | custom-call | tf_op jit(solution)/shard_map/pallas_call | solution.py:599
  17.5 1.1 %shard_map.138 = (f32[64,8,256]{2,1,0:T(8,128)}, f32[64,8,256]{2,1,0:T(8,128)}, f32[8,256]{1,0:T(8,128)}, f32[8,256]{1,0:T(8,128)}, f32[8,256]{1,0:T(8,128)}) custom-call(f32[8,64,256]{2,1,0:T(8,128)S(1)} %get-tuple-element.8.t, f32[8,64,256]{2,1,0:T(8,128)S(1)} %get-tuple-element.9.s, f32[3,8,256]{2,1,0:T(8,128)S(1)} %get-tuple-element.10.surface), custom_call_target="tpu_custom_call" | custom-call | tf_op jit(solution)/shard_map/pallas_call | solution.py:634
